TPU v7x, 1024 devices: a whole 4x8x16 slice. The times are simulated.
1024 devices in a mesh: table: 64 (over y, x, core), sample: 16 (over z).
Axes of the slice: x: 4, y: 8, z: 16, core: 2. Of those that a mesh axis runs over, the one named last changes fastest.
Arguments:
- hist_ids: int32 [16384, 64, 48], P(('table', 'sample')), may hold values from 0 to 2047
- hist_lens: int32 [16384, 64], P(('table', 'sample')), may hold values from 1 to 48, 2048 in all within a row
- table_rows: bfloat16 [131072, 256], P('table'), may hold values from -6 to 6
- imp_user: int32 [262144], P(('table', 'sample')), may hold values from 0 to 255
- item_rows: bfloat16 [262144, 256], P(('table', 'sample')), may hold values from -6 to 6
- labels: int32 [262144], P(('table', 'sample')), may hold values 0 or 1
- w_hidden: bfloat16 [512, 512], replicated, may hold values from -0.25 to 0.25
- b_hidden: float32 [512], replicated, may hold values from -3 to 3
- w_back: bfloat16 [512, 512], replicated, may hold values from -0.25 to 0.25
- w_cross: bfloat16 [512, 512], replicated, may hold values from -0.25 to 0.25
- b_cross: float32 [512], replicated, may hold values from -4 to 4
- norm_gain: float32 [512], replicated, may hold values from 0.25 to 1.75
- w_score: float32 [512], replicated, may hold values from -0.25 to 0.25
Outputs:
- pooled_user: bfloat16 [16384, 256], P(('table', 'sample'))
- scores: float32 [262144], P(('table', 'sample'))
- user_grad: float32 [16384, 256], P(('table', 'sample'))
- item_grad: float32 [262144, 256], P(('table', 'sample'))
Inputs may be any that keep to these rules, and one draw needn't show every extreme that they name: `hist_lens`: each user's live ids over all shards number exactly 2048; some user has 48 live ids in one shard. `imp_user`: an impression names one of the 256 users held by the devices of its own table index.
All inputs are finite; a program needn't handle non-finite values. No bound on the sum of `labels` on one device may be relied on, other than what follows from the above.
Results may differ from a plain program's by a relative error of at most 0.02.
Values may be sent and summed in bfloat16 or wider, within the bound.
No kernel may reach another device: no remote copies, remote signals or barrier semaphores. Data moves between devices by JAX's collectives and lax.ppermute only.
A program may use at most 32 MiB of HBM per device.

v0:
```python
import math

import jax
import jax.numpy as jnp
from jax import lax
from jax.sharding import PartitionSpec as P


def forward(user_in, item_in, w_hidden, b_hidden, w_back, w_cross, b_cross, norm_gain, w_score):
    joined = jnp.concatenate([user_in, item_in], axis=1).astype(jnp.bfloat16)
    hidden = jax.nn.gelu(
        jnp.dot(joined, w_hidden, preferred_element_type=jnp.float32) + b_hidden
    ).astype(jnp.bfloat16)
    mlp_out = jnp.dot(hidden, w_back, preferred_element_type=jnp.float32)
    lifted = joined.astype(jnp.float32)
    crossed = lifted * (jnp.dot(joined, w_cross, preferred_element_type=jnp.float32) + b_cross)
    summed = lifted + mlp_out + crossed
    row_mean = jnp.mean(summed, axis=1, keepdims=True)
    centred = summed - row_mean
    row_var = jnp.mean(centred * centred, axis=1, keepdims=True)
    normed = centred * lax.rsqrt(row_var + 1e-05) * norm_gain
    return jnp.dot(normed, w_score, precision=lax.Precision.HIGHEST)


def body(
    hist_ids,
    hist_lens,
    table_rows,
    imp_user,
    item_rows,
    labels,
    w_hidden,
    b_hidden,
    w_back,
    w_cross,
    b_cross,
    norm_gain,
    w_score,
):
    width = table_rows.shape[1]
    table_count = table_rows.shape[0]
    slot_count = hist_ids.shape[2]
    users_here = hist_ids.shape[0]
    sources = lax.axis_size("table")
    history = slot_count * sources * 2 // 3
    recv_ids = lax.all_to_all(hist_ids, "table", split_axis=1, concat_axis=1, tiled=True)
    recv_lens = lax.all_to_all(hist_lens, "table", split_axis=1, concat_axis=1, tiled=True)
    items = recv_ids.shape[0]
    group = math.gcd(sources, max(1, 128 // max(1, items)))
    blocks_count = sources // group
    flat_ids = jnp.transpose(recv_ids, (1, 0, 2)).reshape(blocks_count, group * items, slot_count)
    flat_lens = jnp.transpose(recv_lens, (1, 0)).reshape(blocks_count, group * items)

    def pool_block(pair):
        block_ids, block_lens = pair
        live_slots = lax.broadcasted_iota(jnp.int32, block_ids.shape, 1) < block_lens[:, None]
        masked_ids = jnp.where(live_slots, block_ids, -1)
        row_iota = lax.broadcasted_iota(jnp.int32, (1, 1, table_count), 2)
        counts = jnp.sum((masked_ids[:, :, None] == row_iota).astype(jnp.float32), axis=1).astype(
            jnp.bfloat16
        )
        return jnp.dot(counts, table_rows, preferred_element_type=jnp.float32)

    pooled_blocks = lax.map(pool_block, (flat_ids, flat_lens))
    partials = jnp.transpose(pooled_blocks.reshape(sources, items, width), (1, 0, 2))
    returned = lax.all_to_all(partials, "table", split_axis=1, concat_axis=1, tiled=True)
    pooled_user = (jnp.sum(returned, axis=1) * float(history) ** (-0.5)).astype(jnp.bfloat16)
    shard_part = lax.all_gather(pooled_user, "sample", axis=0, tiled=True)
    picks = (
        imp_user[:, None] == lax.broadcasted_iota(jnp.int32, (1, shard_part.shape[0]), 1)
    ).astype(jnp.bfloat16)
    expanded = jnp.dot(picks, shard_part, preferred_element_type=jnp.float32)
    user_feat = expanded.astype(jnp.bfloat16)

    def score_of(user_in, item_in):
        return forward(
            user_in, item_in, w_hidden, b_hidden, w_back, w_cross, b_cross, norm_gain, w_score
        )

    scores, pullback = jax.vjp(
        score_of, user_feat.astype(jnp.float32), item_rows.astype(jnp.float32)
    )
    score_grad = jax.nn.sigmoid(scores) - labels.astype(jnp.float32)
    user_part, item_grad = pullback(score_grad)
    group_users = users_here * lax.axis_size("sample")
    picks = (imp_user[:, None] == lax.broadcasted_iota(jnp.int32, (1, group_users), 1)).astype(
        jnp.float32
    )
    per_user = jnp.einsum("ru,re->ue", picks, user_part, precision=lax.Precision.HIGHEST)
    user_grad = lax.psum_scatter(
        per_user.astype(jnp.bfloat16), "sample", scatter_dimension=0, tiled=True
    ).astype(jnp.float32)
    return (pooled_user, scores, user_grad, item_grad)


def solution(mesh):
    in_specs = (
        P(("table", "sample"), None, None),
        P(("table", "sample"), None),
        P("table", None),
        P(("table", "sample")),
        P(("table", "sample"), None),
        P(("table", "sample")),
        P(),
        P(),
        P(),
        P(),
        P(),
        P(),
        P(),
    )
    out_specs = (
        P(("table", "sample"), None),
        P(("table", "sample")),
        P(("table", "sample"), None),
        P(("table", "sample"), None),
    )
    return jax.shard_map(body, mesh=mesh, in_specs=in_specs, out_specs=out_specs, check_vma=False)
```

profile of v0, /device:TPU:6, one launch (start us, length us, event | category | flops | bytes accessed | tf_op | source)
XLA Modules:
  0.0 305.8 jit_solution(11452499882895236973)
XLA Ops:
  7.2 1.5 copy.41
  8.6 17.1 %all-to-all-start = ((s32[16,64,1]{0,2,1:T(1,128)}), s32[16,64,1]{0,2,1:T(1,128)S(1)}, u32[]{:S(2)}, u32[]{:S(2)}) async-start(s32[16,64,1]{0,2,1:T(1,128)} %bitcast.3), calls=%async_computation | async-start | bytes 65536 | tf_op jit(solution)/shard_map/all_to_all | solution.py:47
  25.8 1.3 copy.42
  27.1 1.2 reshape.80
  28.3 5.4 %all-to-all-done = s32[16,64,1]{0,2,1:T(1,128)S(1)} async-done(((s32[16,64,1]{0,2,1:T(1,128)}), s32[16,64,1]{0,2,1:T(1,128)S(1)}, u32[]{:S(2)}, u32[]{:S(2)}) %all-to-all-start) | async-done | bytes 4128 | tf_op jit(solution)/shard_map/all_to_all | solution.py:47
  33.7 6.3 %all-to-all-start.1 = ((s32[64,1,768]{2,1,0:T(1,128)}), s32[64,1,768]{2,1,0:T(1,128)S(1)}, u32[]{:S(2)}, u32[]{:S(2)}) async-start(s32[64,1,768]{2,1,0:T(1,128)} %reshape.80), calls=%async_computation.1 | async-start | bytes 393216 | tf_op jit(solution)/shard_map/all_to_all | solution.py:46
  40.1 10.5 %all-to-all-done.1 = s32[64,1,768]{2,1,0:T(1,128)S(1)} async-done(((s32[64,1,768]{2,1,0:T(1,128)}), s32[64,1,768]{2,1,0:T(1,128)S(1)}, u32[]{:S(2)}, u32[]{:S(2)}) %all-to-all-start.1) | async-done | bytes 196640 | tf_op jit(solution)/shard_map/all_to_all | solution.py:46
  50.6 0.5 broadcast.125
  51.1 1.1 reduce
  52.2 0.3 reshape.81
  52.5 107.5 %while.10 = (s32[]{:T(128)}, f32[8,128,256]{2,1,0:T(8,128)}, s32[8,128]{1,0:T(8,128)S(1)}, s32[8,128,48]{2,1,0:T(8,128)S(1)}, bf16[2048,256]{1,0:T(8,128)(2,1)S(1)}, /*index=5*/s32[]{:T(128)}) while((s32[]{:T(128)}, f32[8,128,256]{2,1,0:T(8,128)}, s32[8,128]{1,0:T(8,128)S(1)}, s32[8,128,48]{2,1,0:T(8,128)S(1)}, ...), condition=%wide.region_2.3_spmd, body=%wide.region_0.2_spmd.sunk | while | flops 171716608 | bytes 2304077 | solution.py:64
  52.6 0.1 bitcast_select_fusion.2
  52.6 12.3 %convert_reduce_fusion.2 = bf16[128,2048]{1,0:T(8,128)(2,1)S(1)} fusion(s32[128,48]{1,0:T(8,128)S(1)} %bitcast_select_fusion.2), kind=kLoop, calls=%fused_computation.clone.1 | loop fusion | flops 37486592 | bytes 548864 | tf_op jit(solution)/shard_map/while/body/eval_jaxpr/reduce_sum | solution.py:59
  65.0 1.0 fusion.85
  66.1 12.3 %convert_reduce_fusion.2 = bf16[128,2048]{1,0:T(8,128)(2,1)S(1)} fusion(s32[128,48]{1,0:T(8,128)S(1)} %bitcast_select_fusion.2), kind=kLoop, calls=%fused_computation.clone.1 | loop fusion | flops 37486592 | bytes 548864 | tf_op jit(solution)/shard_map/while/body/eval_jaxpr/reduce_sum | solution.py:59
  78.4 1.0 fusion.85
  79.5 12.3 %convert_reduce_fusion.2 = bf16[128,2048]{1,0:T(8,128)(2,1)S(1)} fusion(s32[128,48]{1,0:T(8,128)S(1)} %bitcast_select_fusion.2), kind=kLoop, calls=%fused_computation.clone.1 | loop fusion | flops 37486592 | bytes 548864 | tf_op jit(solution)/shard_map/while/body/eval_jaxpr/reduce_sum | solution.py:59
  91.9 1.0 fusion.85
  92.9 12.3 %convert_reduce_fusion.2 = bf16[128,2048]{1,0:T(8,128)(2,1)S(1)} fusion(s32[128,48]{1,0:T(8,128)S(1)} %bitcast_select_fusion.2), kind=kLoop, calls=%fused_computation.clone.1 | loop fusion | flops 37486592 | bytes 548864 | tf_op jit(solution)/shard_map/while/body/eval_jaxpr/reduce_sum | solution.py:59
  105.3 1.0 fusion.85
  106.4 12.3 %convert_reduce_fusion.2 = bf16[128,2048]{1,0:T(8,128)(2,1)S(1)} fusion(s32[128,48]{1,0:T(8,128)S(1)} %bitcast_select_fusion.2), kind=kLoop, calls=%fused_computation.clone.1 | loop fusion | flops 37486592 | bytes 548864 | tf_op jit(solution)/shard_map/while/body/eval_jaxpr/reduce_sum | solution.py:59
  118.7 1.0 fusion.85
  119.8 12.3 %convert_reduce_fusion.2 = bf16[128,2048]{1,0:T(8,128)(2,1)S(1)} fusion(s32[128,48]{1,0:T(8,128)S(1)} %bitcast_select_fusion.2), kind=kLoop, calls=%fused_computation.clone.1 | loop fusion | flops 37486592 | bytes 548864 | tf_op jit(solution)/shard_map/while/body/eval_jaxpr/reduce_sum | solution.py:59
  132.1 1.0 fusion.85
  133.2 12.3 %convert_reduce_fusion.2 = bf16[128,2048]{1,0:T(8,128)(2,1)S(1)} fusion(s32[128,48]{1,0:T(8,128)S(1)} %bitcast_select_fusion.2), kind=kLoop, calls=%fused_computation.clone.1 | loop fusion | flops 37486592 | bytes 548864 | tf_op jit(solution)/shard_map/while/body/eval_jaxpr/reduce_sum | solution.py:59
  145.6 1.0 fusion.85
  146.7 12.3 %convert_reduce_fusion.2 = bf16[128,2048]{1,0:T(8,128)(2,1)S(1)} fusion(s32[128,48]{1,0:T(8,128)S(1)} %bitcast_select_fusion.2), kind=kLoop, calls=%fused_computation.clone.1 | loop fusion | flops 37486592 | bytes 548864 | tf_op jit(solution)/shard_map/while/body/eval_jaxpr/reduce_sum | solution.py:59
  159.0 1.0 fusion.85
  160.0 6.2 %all-to-all-start.2 = ((f32[16,64,256]{2,0,1:T(8,128)}), f32[16,64,256]{2,0,1:T(8,128)S(1)}, u32[]{:S(2)}, u32[]{:S(2)}) async-start(f32[16,64,256]{2,0,1:T(8,128)} %bitcast.9), calls=%async_computation.2 | async-start | bytes 2097152 | tf_op jit(solution)/shard_map/all_to_all | solution.py:66
  166.3 0.1 copy.43
  166.4 28.7 %all-to-all-done.2 = f32[16,64,256]{2,0,1:T(8,128)S(1)} async-done(((f32[16,64,256]{2,0,1:T(8,128)}), f32[16,64,256]{2,0,1:T(8,128)S(1)}, u32[]{:S(2)}, u32[]{:S(2)}) %all-to-all-start.2) | async-done | bytes 1048608 | tf_op jit(solution)/shard_map/all_to_all | solution.py:66
  195.1 0.1 reduce_sum.52
  195.2 36.4 %all_gather.3 = bf16[256,256]{1,0:T(8,128)(2,1)S(1)} all-gather(bf16[16,256]{1,0:T(8,128)(2,1)S(1)} %multiply_convert_fusion.2), channel_id=1, replica_groups=mesh['table'=64,'sample'=16] {'sample'}, dimensions={0}, use_global_device_ids=true | all-gather | bytes 139264 | tf_op jit(solution)/shard_map/all_gather | solution.py:68
  231.7 0.3 convolution_convert_fusion.4
  232.0 0.4 convolution_add_fusion
  232.4 0.3 convolution_add_fusion.2
  232.8 0.5 fusion.67
  233.3 0.1 multiply_reduce_fusion.1
  233.4 0.4 fusion.24
  233.9 0.1 copy-done.12
  233.9 0.2 multiply_reduce_fusion
  234.2 0.2 fusion.66
  234.4 0.5 fusion.5
  235.0 1.0 fusion.6
  236.0 1.0 convolution_convert_fusion.3
  237.0 0.8 copy.48
  237.9 59.8 %reduce-scatter.2.cloned.1.call-done = bf16[16,256]{1,0:T(8,128)(2,1)} async-done(((bf16[256,256]{1,0:T(8,128)(2,1)}), bf16[16,256]{1,0:T(8,128)(2,1)}) %reduce-scatter.2.cloned.1.call-update) | async-done | bytes 8208 | tf_op jit(solution)/shard_map/reduce_scatter | solution.py:90
  297.7 1.3 convert_element_type.59
  (51 shorter events, 0.9 us)
Async XLA Ops:
  7.2 225.6 %copy-start = (bf16[512,512]{1,0:T(8,128)(2,1)S(1)}, bf16[512,512]{1,0:T(8,128)(2,1)}, u32[]{:S(2)}) copy-start(bf16[512,512]{1,0:T(8,128)(2,1)} %param.23) | copy-start | bytes 1572868
  8.6 25.1 %all-to-all-start = ((s32[16,64,1]{0,2,1:T(1,128)}), s32[16,64,1]{0,2,1:T(1,128)S(1)}, u32[]{:S(2)}, u32[]{:S(2)}) async-start(s32[16,64,1]{0,2,1:T(1,128)} %bitcast.3), calls=%async_computation | async-start | bytes 65536 | tf_op jit(solution)/shard_map/all_to_all | solution.py:47
  27.1 25.5 %copy-start.1 = (bf16[2048,256]{1,0:T(8,128)(2,1)S(1)}, bf16[2048,256]{1,0:T(8,128)(2,1)}, u32[]{:S(2)}) copy-start(bf16[2048,256]{1,0:T(8,128)(2,1)} %param.17) | copy-start | bytes 3145732
  33.7 16.9 %all-to-all-start.1 = ((s32[64,1,768]{2,1,0:T(1,128)}), s32[64,1,768]{2,1,0:T(1,128)S(1)}, u32[]{:S(2)}, u32[]{:S(2)}) async-start(s32[64,1,768]{2,1,0:T(1,128)} %reshape.80), calls=%async_computation.1 | async-start | bytes 393216 | tf_op jit(solution)/shard_map/all_to_all | solution.py:46
  160.0 6.3 %copy-start.4 = (bf16[256,256]{1,0:T(8,128)(2,1)S(1)}, bf16[256,256]{1,0:T(8,128)(2,1)}, u32[]{:S(2)}) copy-start(bf16[256,256]{1,0:T(8,128)(2,1)} %param.19) | copy-start | bytes 393220
  160.0 35.1 %all-to-all-start.2 = ((f32[16,64,256]{2,0,1:T(8,128)}), f32[16,64,256]{2,0,1:T(8,128)S(1)}, u32[]{:S(2)}, u32[]{:S(2)}) async-start(f32[16,64,256]{2,0,1:T(8,128)} %bitcast.9), calls=%async_computation.2 | async-start | bytes 2097152 | tf_op jit(solution)/shard_map/all_to_all | solution.py:66
  166.2 65.5 %copy-start.11 = (s32[256]{0:T(256)S(1)}, s32[256]{0:T(256)}, u32[]{:S(2)}) copy-start(s32[256]{0:T(256)} %param.18) | copy-start | bytes 3076
  166.2 65.8 %copy-start.2 = (bf16[512,512]{1,0:T(8,128)(2,1)S(1)}, bf16[512,512]{1,0:T(8,128)(2,1)}, u32[]{:S(2)}) copy-start(bf16[512,512]{1,0:T(8,128)(2,1)} %param.24) | copy-start | bytes 1572868
  166.2 65.8 %copy-start.9 = (f32[512]{0:T(512)S(1)}, f32[512]{0:T(512)}, u32[]{:S(2)}) copy-start(f32[512]{0:T(512)} %param.25) | copy-start | bytes 6148
  166.2 131.5 %reduce-scatter.2.cloned.1.call-start = ((), (), s32[]{:S(2)}) async-start(), calls=%async_computation.4 | async-start | bytes 139264 | tf_op jit(solution)/shard_map/reduce_scatter | solution.py:90
  195.2 37.2 %copy-start.3 = (bf16[512,512]{1,0:T(8,128)(2,1)S(1)}, bf16[512,512]{1,0:T(8,128)(2,1)}, u32[]{:S(2)}) copy-start(bf16[512,512]{1,0:T(8,128)(2,1)} %param.21) | copy-start | bytes 1572868
  195.2 37.2 %copy-start.10 = (f32[512]{0:T(512)S(1)}, f32[512]{0:T(512)}, u32[]{:S(2)}) copy-start(f32[512]{0:T(512)} %param.22) | copy-start | bytes 6148
  195.2 37.5 %copy-start.5 = (bf16[16,256]{1,0:T(8,128)(2,1)}, bf16[16,256]{1,0:T(8,128)(2,1)S(1)}, u32[]{:S(2)}) copy-start(bf16[16,256]{1,0:T(8,128)(2,1)S(1)} %multiply_convert_fusion.2) | copy-start | bytes 24580
  232.7 0.7 copy-start.6
  232.8 0.7 copy-start.7
  233.3 0.7 copy-start.12
  233.9 1.1 copy-start.8
Sparse Core Ops, SparseCore 0:
  237.1 60.5 reduce-scatter.1
where the time goes:
time: 307 us; the launch traced here: 306 us
  waiting for transfers between devices  105 us (34%)
  other arithmetic  103 us (34%)
  blocking collectives  36.4 us (12%)
  starting transfers between devices  29.6 us (10%)
  between operations  14.3 us (5%)
  matrix products  12.2 us (4%)
  local copies, waits for them, and re-layouts  5.96 us (2%)
    reduce_sum x8, other arithmetic, pool_block(): jnp.sum((masked_ids[:, :, None] == row_iota).astype(jnp.float32), axis=1)  98.8 us
    reduce_scatter x1, waiting for transfers between devices, body(): lax.psum_scatter(per_user.astype(jnp.bfloat16), 'sample', scatter_dimensi...  59.8 us
    all_gather x1, blocking collectives, body(): shard_part = lax.all_gather(pooled_user, 'sample', axis=0, tiled=True)  36.4 us
    all_to_all x1, waiting for transfers between devices, body(): lax.all_to_all(partials, 'table', split_axis=1, concat_axis=1, tiled=True)  28.7 us
    all_to_all x1, starting transfers between devices, body(): lax.all_to_all(hist_lens, 'table', split_axis=1, concat_axis=1, tiled=True)  17.1 us
    all_to_all x1, waiting for transfers between devices, body(): lax.all_to_all(hist_ids, 'table', split_axis=1, concat_axis=1, tiled=True)  10.5 us
    dot_general x8, matrix products, pool_block(): return jnp.dot(counts, table_rows, preferred_element_type=jnp.float32)  7.81 us
    all_to_all x1, starting transfers between devices, body(): lax.all_to_all(hist_ids, 'table', split_axis=1, concat_axis=1, tiled=True)  6.28 us
  transfers between devices with their start and end apart: 4, of which 4 were waited for; matrix products, arithmetic and copies ran while one was open for 1% of the time, Pallas kernels for 0%

commit v1 on v0

v1 whole, which is shorter than its diff:
```python
import jax
import jax.numpy as jnp
from jax import lax
from jax.experimental import pallas as pl
from jax.experimental.pallas import tpu as pltpu
from jax.sharding import PartitionSpec as P

F32 = jnp.float32
BF16 = jnp.bfloat16
LOW = 256
VMEM_LIMIT = 48 * 1024 * 1024


def rows_by_rows(a, b):
    return lax.dot_general(a, b, (((1,), (1,)), ((), ())), preferred_element_type=F32)


def pack_kernel(ids_ref, lens_ref, out_ref):
    users, slots, shards = ids_ref.shape
    ids = ids_ref[...]
    live = lax.broadcasted_iota(jnp.int32, ids.shape, 1) < lens_ref[...][:, None, :]
    ids = jnp.where(live, ids, -1)
    half = users // 2
    words = (ids[:half] & 0xFFFF) | (ids[half:] << 16)
    out_ref[...] = words.reshape(half * slots, shards).T.reshape(out_ref.shape)


def pool_kernel(users, words_ref, table_ref, out_ref, counts_ref):
    sources = words_ref.shape[0]
    positions = 2 * words_ref.shape[2]
    highs = counts_ref.shape[0]
    slots = positions // users
    user_of = lax.broadcasted_iota(jnp.int32, (1, positions), 1) // slots
    high_rows = lax.broadcasted_iota(jnp.int32, (highs * users, positions), 0).astype(F32).astype(BF16)
    low_rows = lax.broadcasted_iota(jnp.int32, (LOW, positions), 0).astype(F32).astype(BF16)
    one, zero = jnp.ones((), BF16), jnp.zeros((), BF16)

    def count(source, carry):
        words = words_ref[source]
        ids = jnp.concatenate([words & 0xFFFF, (words >> 16) & 0xFFFF], axis=1)
        high = ((ids // LOW) * users + user_of).astype(F32).astype(BF16)
        low = (ids % LOW).astype(F32).astype(BF16)
        high_hot = jnp.where(high == high_rows, one, zero)
        low_hot = jnp.where(low == low_rows, one, zero)
        counts = rows_by_rows(high_hot, low_hot).astype(BF16)
        rows = pl.ds(pl.multiple_of(source * users, users), users)
        for part in range(highs):
            counts_ref[part, rows, :] = counts[part * users : (part + 1) * users]
        return carry

    lax.fori_loop(0, sources, count, 0, unroll=2)

    chunk = 16
    for first in range(0, sources, chunk):
        total = None
        for part in range(highs):
            term = jnp.dot(
                counts_ref[part, first * users : (first + chunk) * users, :],
                table_ref[part * LOW : (part + 1) * LOW, :],
                preferred_element_type=F32,
            )
            total = term if total is None else total + term
        out_ref[first : first + chunk] = total.astype(BF16).reshape(chunk, users, total.shape[1])


def dense_kernel(
    rows_ref,
    imp_ref,
    item_ref,
    labels_ref,
    w_hidden_ref,
    b_hidden_ref,
    w_back_ref,
    w_cross_ref,
    b_cross_ref,
    gain_ref,
    w_score_ref,
    scores_ref,
    item_grad_ref,
    per_user_ref,
):
    group_users, width = rows_ref.shape
    imps = item_ref.shape[0]
    picks_t = jnp.where(
        lax.broadcasted_iota(jnp.int32, (group_users, imps), 0) == imp_ref[...], 1.0, 0.0
    ).astype(F32)
    picks = picks_t.T.astype(BF16)
    picks_t = picks_t.astype(BF16)
    user_feat = jnp.dot(picks, rows_ref[...], preferred_element_type=F32).astype(BF16)
    joined = jnp.concatenate([user_feat, item_ref[...]], axis=1)
    lifted = joined.astype(F32)
    pre = jnp.dot(joined, w_hidden_ref[...], preferred_element_type=F32) + b_hidden_ref[...]
    cross = jnp.dot(joined, w_cross_ref[...], preferred_element_type=F32) + b_cross_ref[...]
    k, c = 0.7978845608028654, 0.044715
    square = pre * pre
    tanh = jnp.tanh(k * pre * (1.0 + c * square))
    cdf = 0.5 * (1.0 + tanh)
    hidden = (pre * cdf).astype(BF16)
    slope = cdf + 0.5 * pre * (1.0 - tanh * tanh) * (k * (1.0 + 3.0 * c * square))
    summed = lifted + jnp.dot(hidden, w_back_ref[...], preferred_element_type=F32) + lifted * cross
    columns = summed.shape[1]
    centred = summed - jnp.sum(summed, axis=1, keepdims=True) * (1.0 / columns)
    variance = jnp.sum(centred * centred, axis=1, keepdims=True) * (1.0 / columns)
    scale = lax.rsqrt(variance + 1e-05)
    weight = gain_ref[...] * w_score_ref[...]
    scores = scale * jnp.sum(centred * weight, axis=1, keepdims=True)
    scores_ref[...] = jnp.broadcast_to(scores, (imps, 128)).T[:1]
    labels = jnp.broadcast_to(labels_ref[...].astype(F32), (8, imps)).T[:, :1]
    score_grad = 1.0 / (1.0 + jnp.exp(-scores)) - labels
    flat = weight - jnp.sum(weight, axis=1, keepdims=True) * (1.0 / columns)
    summed_grad = (score_grad * scale) * (flat - centred * (scale * scores * (1.0 / columns)))
    hidden_grad = rows_by_rows(summed_grad.astype(BF16), w_back_ref[...])
    pre_grad = (hidden_grad * slope).astype(BF16)
    cross_grad = (summed_grad * lifted).astype(BF16)
    joined_grad = (
        summed_grad * (1.0 + cross)
        + rows_by_rows(pre_grad, w_hidden_ref[...])
        + rows_by_rows(cross_grad, w_cross_ref[...])
    )
    item_grad_ref[...] = joined_grad[:, width:]
    user_part = joined_grad[:, :width].astype(BF16)
    per_user_ref[...] = jnp.dot(picks_t, user_part, preferred_element_type=F32).astype(BF16)


def kernel_call(kernel, out_shape, flops, scratch=()):
    return pl.pallas_call(
        kernel,
        out_shape=out_shape,
        scratch_shapes=list(scratch),
        compiler_params=pltpu.CompilerParams(vmem_limit_bytes=VMEM_LIMIT),
        cost_estimate=pl.CostEstimate(flops=flops, bytes_accessed=1 << 21, transcendentals=0),
    )


def body(
    hist_ids,
    hist_lens,
    table_rows,
    imp_user,
    item_rows,
    labels,
    w_hidden,
    b_hidden,
    w_back,
    w_cross,
    b_cross,
    norm_gain,
    w_score,
):
    users, sources, slots = hist_ids.shape
    table_count, width = table_rows.shape
    samples = lax.axis_size("sample")
    imps = imp_user.shape[0]
    history = slots * sources * 2 // 3
    with jax.named_scope("pack_ids"):
        words = kernel_call(
            pack_kernel,
            jax.ShapeDtypeStruct((sources, 1, users * slots // 2), jnp.int32),
            1 << 20,
        )(jnp.transpose(hist_ids, (0, 2, 1)), hist_lens)
    words = lax.all_to_all(words, "table", split_axis=0, concat_axis=0, tiled=True)
    with jax.named_scope("pool"):
        partials = kernel_call(
            lambda *refs: pool_kernel(users, *refs),
            jax.ShapeDtypeStruct((sources, users, width), BF16),
            1 << 32,
            [pltpu.VMEM((table_count // LOW, sources * users, LOW), BF16)],
        )(words, table_rows)
    returned = lax.all_to_all(partials, "table", split_axis=0, concat_axis=0, tiled=True)
    pooled_user = (jnp.sum(returned.astype(F32), axis=0) * float(history) ** (-0.5)).astype(BF16)
    group_rows = lax.all_to_all(
        jnp.broadcast_to(pooled_user[None], (samples, users, width)),
        "sample",
        split_axis=0,
        concat_axis=0,
        tiled=True,
    ).reshape(samples * users, width)
    row = lambda vector: vector.reshape(1, -1)
    with jax.named_scope("dense"):
        scores, item_grad, per_user = kernel_call(
            dense_kernel,
            (
                jax.ShapeDtypeStruct((1, imps), F32),
                jax.ShapeDtypeStruct((imps, width), F32),
                jax.ShapeDtypeStruct((samples * users, width), BF16),
            ),
            1 << 30,
        )(
            group_rows,
            row(imp_user),
            item_rows,
            row(labels),
            w_hidden,
            row(b_hidden),
            w_back,
            w_cross,
            row(b_cross),
            row(norm_gain),
            row(w_score),
        )
    parts = lax.all_to_all(
        per_user.reshape(samples, users, width), "sample", split_axis=0, concat_axis=0, tiled=True
    )
    user_grad = jnp.sum(parts.astype(F32), axis=0)
    return (pooled_user, scores.reshape(-1), user_grad, item_grad)


def solution(mesh):
    both = ("table", "sample")
    in_specs = (
        P(both, None, None),
        P(both, None),
        P("table", None),
        P(both),
        P(both, None),
        P(both),
    ) + (P(),) * 7
    out_specs = (P(both, None), P(both), P(both, None), P(both, None))
    return jax.shard_map(body, mesh=mesh, in_specs=in_specs, out_specs=out_specs, check_vma=False)
```

time: 307 us -> 117 us (0.38)
  the two profiles are of different devices: /device:TPU:6 before, /device:TPU:8 now
where the time goes in v1:
time: 117 us
  blocking collectives  94.1 us (80%)
  Pallas kernels  17.2 us (15%)
  local copies, waits for them, and re-layouts  4.16 us (4%)
    all_to_all x1, blocking collectives, body(): lax.all_to_all(jnp.broadcast_to(pooled_user[None], (samples, users, width...  26.7 us
    all_to_all x1, blocking collectives, body(): lax.all_to_all(words, 'table', split_axis=0, concat_axis=0, tiled=True)  26 us
    all_to_all x1, blocking collectives, body(): lax.all_to_all(partials, 'table', split_axis=0, concat_axis=0, tiled=True)  21.7 us
    all_to_all x1, blocking collectives, body(): lax.all_to_all(per_user.reshape(samples, users, width), 'sample', split_a...  19.7 us
    pallas_call x1, Pallas kernels, body(): kernel_call(lambda *refs: pool_kernel(users, *refs), jax.ShapeDtypeStruct...  14.6 us
    unnamed x28, local copies, waits for them, and re-layouts  4.15 us
    pallas_call x1, Pallas kernels, body(): kernel_call(dense_kernel, (jax.ShapeDtypeStruct((1, imps), F32), jax.Shap...  2.51 us

profile of v1, /device:TPU:8, one launch (start us, length us, event | category | flops | bytes accessed | tf_op | source)
XLA Modules:
  0.0 116.9 jit_solution(15087641339330096011)
XLA Ops:
  0.6 0.0 copy-start
  0.6 1.0 copy-done
  1.6 0.0 copy-start.1
  1.6 0.7 copy-done.1
  2.3 0.1 pack_ids.1
  2.5 26.0 %all_to_all.20.refs_0_ = s32[64,1,384]{2,1,0:T(1,128)S(1)} all-to-all(s32[64,1,384]{2,1,0:T(1,128)S(1)} %pack_ids.1), channel_id=1, replica_groups=mesh['table'=64,'sample'=16] {'table'}, dimensions={0} | all-to-all | bytes 196608 | tf_op jit(solution)/shard_map/all_to_all | solution.py:161
  28.5 0.0 copy-start.2
  28.5 1.2 %copy-done.2 = bf16[2048,256]{1,0:T(8,128)(2,1)S(1)} copy-done((bf16[2048,256]{1,0:T(8,128)(2,1)S(1)}, bf16[2048,256]{1,0:T(8,128)(2,1)}, u32[]{:S(2)}) %copy-start.2) | copy-done | bytes 1048600
  29.7 14.6 %pool.1 = bf16[64,16,256]{2,1,0:T(8,128)(2,1)S(1)} custom-call(s32[64,1,384]{2,1,0:T(1,128)S(1)} %all_to_all.20.refs_0_, bf16[2048,256]{1,0:T(8,128)(2,1)S(1)} %copy-done.2), custom_call_target="tpu_custom_call" | custom-call | flops 4294967296 | bytes 2097152 | tf_op jit(solution)/shard_map/pool/pallas_call | solution.py:163
  44.3 0.0 copy-start.4
  44.3 0.0 copy-start.5
  44.3 21.7 %all_to_all.21 = bf16[64,16,256]{2,1,0:T(8,128)(2,1)S(1)} all-to-all(bf16[64,16,256]{2,1,0:T(8,128)(2,1)S(1)} %pool.1), channel_id=1, replica_groups=mesh['table'=64,'sample'=16] {'table'}, dimensions={0} | all-to-all | bytes 1048576 | tf_op jit(solution)/shard_map/all_to_all | solution.py:169
  66.0 0.0 copy-start.3
  66.0 0.1 convert_reduce_fusion
  66.1 0.0 copy-start.13
  66.1 0.6 copy-done.13
  66.7 0.0 copy-start.6
  66.7 0.0 copy-start.8
  66.7 0.0 copy-start.9
  66.7 0.0 copy-start.10
  66.7 0.0 copy-start.12
  66.7 26.7 %all_to_all.22 = bf16[16,16,256]{2,1,0:T(8,128)(2,1)S(1)} all-to-all(bf16[16,16,256]{2,1,0:T(8,128)(2,1)S(1)} %broadcast_in_dim.2), channel_id=1, replica_groups=mesh['table'=64,'sample'=16] {'sample'}, dimensions={0} | all-to-all | bytes 262144 | tf_op jit(solution)/shard_map/all_to_all | solution.py:171
  93.4 0.0 copy-start.7
  93.4 0.0 copy-start.11
  93.4 0.0 copy-done.4
  93.4 0.0 copy-done.5
  93.4 0.0 copy-done.3
  93.4 0.0 copy-done.6
  93.4 0.0 copy-done.8
  93.4 0.0 copy-done.9
  93.5 0.0 copy-done.10
  93.5 0.0 copy-done.12
  93.5 0.6 copy-done.7
  94.1 0.0 copy-done.11
  94.1 2.5 %dense.1 = (f32[1,256]{1,0:T(1,128)}, f32[256,256]{1,0:T(8,128)}, bf16[256,256]{1,0:T(8,128)(2,1)S(1)}) custom-call(bf16[256,256]{1,0:T(8,128)(2,1)S(1)} %bitcast.11, s32[1,256]{1,0:T(1,128)S(1)} %bitcast.17, bf16[256,256]{1,0:T(8,128)(2,1)S(1)} %copy-done.6, s32[1,256]{1,0:T(1,128)S(1)} %bitcast.18, bf16[512,512]{1,0:T(8,128)(2,1)S(1)} %copy-done.3, ...), custom_call_target="tpu_custom_call" | custom-call | flops 1073741824 | bytes 2097152 | tf_op jit(solution)/shard_map/dense/pallas_call | solution.py:180
  96.6 19.7 %all_to_all.23 = bf16[16,16,256]{2,1,0:T(8,128)(2,1)S(1)} all-to-all(bf16[16,16,256]{2,1,0:T(8,128)(2,1)S(1)} %bitcast.12), channel_id=1, replica_groups=mesh['table'=64,'sample'=16] {'sample'}, dimensions={0} | all-to-all | bytes 262144 | tf_op jit(solution)/shard_map/all_to_all | solution.py:201
  116.3 0.6 convert_reduce_fusion.1
  (2 shorter events, 0.0 us)
Async XLA Ops:
  0.6 1.0 copy-start
  1.6 0.7 copy-start.1
  28.5 1.2 %copy-start.2 = (bf16[2048,256]{1,0:T(8,128)(2,1)S(1)}, bf16[2048,256]{1,0:T(8,128)(2,1)}, u32[]{:S(2)}) copy-start(bf16[2048,256]{1,0:T(8,128)(2,1)} %refs_1_.1) | copy-start | bytes 3145732
  44.3 49.2 %copy-start.4 = (bf16[512,512]{1,0:T(8,128)(2,1)S(1)}, bf16[512,512]{1,0:T(8,128)(2,1)}, u32[]{:S(2)}) copy-start(bf16[512,512]{1,0:T(8,128)(2,1)} %w_back_ref.1) | copy-start | bytes 1572868
  44.3 49.1 %copy-start.5 = (bf16[512,512]{1,0:T(8,128)(2,1)S(1)}, bf16[512,512]{1,0:T(8,128)(2,1)}, u32[]{:S(2)}) copy-start(bf16[512,512]{1,0:T(8,128)(2,1)} %w_cross_ref.1) | copy-start | bytes 1572868
  66.0 27.4 %copy-start.3 = (bf16[512,512]{1,0:T(8,128)(2,1)S(1)}, bf16[512,512]{1,0:T(8,128)(2,1)}, u32[]{:S(2)}) copy-start(bf16[512,512]{1,0:T(8,128)(2,1)} %w_hidden_ref.1) | copy-start | bytes 1572868
  66.1 0.6 copy-start.13
  66.7 26.7 %copy-start.6 = (bf16[256,256]{1,0:T(8,128)(2,1)S(1)}, bf16[256,256]{1,0:T(8,128)(2,1)}, u32[]{:S(2)}) copy-start(bf16[256,256]{1,0:T(8,128)(2,1)} %item_ref.1) | copy-start | bytes 393220
  66.7 26.7 %copy-start.8 = (f32[512]{0:T(512)S(1)}, f32[512]{0:T(512)}, u32[]{:S(2)}) copy-start(f32[512]{0:T(512)} %param.23) | copy-start | bytes 6148
  66.7 26.7 %copy-start.9 = (f32[512]{0:T(512)S(1)}, f32[512]{0:T(512)}, u32[]{:S(2)}) copy-start(f32[512]{0:T(512)} %param.24) | copy-start | bytes 6148
  66.7 26.8 %copy-start.10 = (f32[512]{0:T(512)S(1)}, f32[512]{0:T(512)}, u32[]{:S(2)}) copy-start(f32[512]{0:T(512)} %param.25) | copy-start | bytes 6148
  66.7 26.8 %copy-start.12 = (s32[256]{0:T(256)S(1)}, s32[256]{0:T(256)}, u32[]{:S(2)}) copy-start(s32[256]{0:T(256)} %param.18) | copy-start | bytes 3076
  93.4 0.7 copy-start.7
  93.4 0.7 copy-start.11

commit v2 on v1

--- a/solution.py
+++ b/solution.py
@@ -7,6 +7,7 @@
 
 F32 = jnp.float32
 BF16 = jnp.bfloat16
+F8 = jnp.float8_e4m3fn
 LOW = 256
 VMEM_LIMIT = 48 * 1024 * 1024
 
@@ -15,48 +16,68 @@
     return lax.dot_general(a, b, (((1,), (1,)), ((), ())), preferred_element_type=F32)
 
 
-def pack_kernel(ids_ref, lens_ref, out_ref):
-    users, slots, shards = ids_ref.shape
-    ids = ids_ref[...]
-    live = lax.broadcasted_iota(jnp.int32, ids.shape, 1) < lens_ref[...][:, None, :]
+def pack_words(ids, lens):
+    live = lax.broadcasted_iota(jnp.int32, ids.shape, 1) < lens[:, None, :]
     ids = jnp.where(live, ids, -1)
-    half = users // 2
-    words = (ids[:half] & 0xFFFF) | (ids[half:] << 16)
-    out_ref[...] = words.reshape(half * slots, shards).T.reshape(out_ref.shape)
-
-
-def pool_kernel(users, words_ref, table_ref, out_ref, counts_ref):
+    half = ids.shape[0] // 2
+    return (ids[:half] & 0xFFFF) | (ids[half:] << 16)
+
+
+def turn_kernel(words_ref, out_ref):
+    half, slots, shards = words_ref.shape
+    words = words_ref[...].reshape(half * slots, shards).T
+    chips, cores, _ = out_ref.shape
+    for chip in range(chips):
+        out_ref[chip] = words[chip * cores : (chip + 1) * cores]
+
+
+def pool_kernel(users, n_staged, words_ref, other_ref, table_hbm, *refs):
+    staged_hbm, (out_ref, *staged_refs) = refs[:n_staged], refs[n_staged : 2 * n_staged + 1]
+    counts_ref, table_ref, sems = refs[2 * n_staged + 1 :]
+    copies = [pltpu.make_async_copy(table_hbm, table_ref, sems.at[0])]
+    for i, (source, target) in enumerate(zip(staged_hbm, staged_refs)):
+        copies.append(pltpu.make_async_copy(source, target, sems.at[i + 1]))
+    for copy in copies:
+        copy.start()
     sources = words_ref.shape[0]
+    first_core = lax.rem(lax.axis_index("table"), 2) == 0
     positions = 2 * words_ref.shape[2]
-    highs = counts_ref.shape[0]
+    highs = table_ref.shape[0] // LOW
     slots = positions // users
     user_of = lax.broadcasted_iota(jnp.int32, (1, positions), 1) // slots
-    high_rows = lax.broadcasted_iota(jnp.int32, (highs * users, positions), 0).astype(F32).astype(BF16)
-    low_rows = lax.broadcasted_iota(jnp.int32, (LOW, positions), 0).astype(F32).astype(BF16)
-    one, zero = jnp.ones((), BF16), jnp.zeros((), BF16)
+    high_rows = lax.broadcasted_iota(jnp.int32, (highs * users, positions), 0).astype(jnp.int8)
+    low_rows = (lax.broadcasted_iota(jnp.int32, (LOW, positions), 0) - LOW // 2).astype(jnp.int8)
+    one, zero = jnp.ones((), F8), jnp.zeros((), F8)
 
     def count(source, carry):
-        words = words_ref[source]
-        ids = jnp.concatenate([words & 0xFFFF, (words >> 16) & 0xFFFF], axis=1)
-        high = ((ids // LOW) * users + user_of).astype(F32).astype(BF16)
-        low = (ids % LOW).astype(F32).astype(BF16)
-        high_hot = jnp.where(high == high_rows, one, zero)
-        low_hot = jnp.where(low == low_rows, one, zero)
-        counts = rows_by_rows(high_hot, low_hot).astype(BF16)
+        pair = words_ref[source]
+        own = jnp.where(first_core, pair[:1], pair[1:])
+        other = jnp.where(first_core, pair[1:], pair[:1])
         rows = pl.ds(pl.multiple_of(source * users, users), users)
-        for part in range(highs):
-            counts_ref[part, rows, :] = counts[part * users : (part + 1) * users]
+        for shard, words in enumerate((own, other)):
+            ids = jnp.concatenate([words & 0xFFFF, (words >> 16) & 0xFFFF], axis=1)
+            high = (ids // LOW) * users + user_of
+            high = jnp.where(high < highs * users, high, -1).astype(jnp.int8)
+            low = (ids % LOW - LOW // 2).astype(jnp.int8)
+            high_hot = jnp.where(high == high_rows, one, zero)
+            low_hot = jnp.where(low == low_rows, one, zero)
+            counts = rows_by_rows(high_hot, low_hot).astype(BF16)
+            for part in range(highs):
+                counts_ref[shard * highs + part, rows, :] = counts[part * users : (part + 1) * users]
         return carry
 
-    lax.fori_loop(0, sources, count, 0, unroll=2)
-
+    lax.fori_loop(0, sources, count, 0, unroll=8)
+    for copy in copies:
+        copy.wait()
     chunk = 16
     for first in range(0, sources, chunk):
         total = None
-        for part in range(highs):
+        for part in range(2 * highs):
+            shard_ref = (table_ref, other_ref)[part // highs]
+            low_row = part % highs * LOW
             term = jnp.dot(
                 counts_ref[part, first * users : (first + chunk) * users, :],
-                table_ref[part * LOW : (part + 1) * LOW, :],
+                shard_ref[low_row : low_row + LOW, :],
                 preferred_element_type=F32,
             )
             total = term if total is None else total + term
@@ -122,13 +143,38 @@
     per_user_ref[...] = jnp.dot(picks_t, user_part, preferred_element_type=F32).astype(BF16)
 
 
-def kernel_call(kernel, out_shape, flops, scratch=()):
+def finish_kernel(parts_ref, item_ref, scores_ref, pooled_ref, user_hbm, item_hbm, scores_hbm, pooled_hbm, sums_ref, sems):
+    copies = [
+        pltpu.make_async_copy(item_ref, item_hbm, sems.at[0]),
+        pltpu.make_async_copy(scores_ref, scores_hbm, sems.at[1]),
+        pltpu.make_async_copy(pooled_ref, pooled_hbm, sems.at[2]),
+    ]
+    for copy in copies:
+        copy.start()
+    sums_ref[...] = jnp.sum(parts_ref[...].astype(F32), axis=0)
+    copies.append(pltpu.make_async_copy(sums_ref, user_hbm, sems.at[3]))
+    copies[-1].start()
+    for copy in copies:
+        copy.wait()
+
+
+HBM = pl.BlockSpec(memory_space=pltpu.HBM)
+VMEM = pl.BlockSpec(memory_space=pltpu.VMEM)
+
+
+def kernel_call(kernel, out_shape, flops, in_specs=None, out_specs=None, scratch=()):
+    specs = {}
+    if in_specs is not None:
+        specs["in_specs"] = in_specs
+    if out_specs is not None:
+        specs["out_specs"] = out_specs
     return pl.pallas_call(
         kernel,
         out_shape=out_shape,
         scratch_shapes=list(scratch),
         compiler_params=pltpu.CompilerParams(vmem_limit_bytes=VMEM_LIMIT),
         cost_estimate=pl.CostEstimate(flops=flops, bytes_accessed=1 << 21, transcendentals=0),
+        **specs,
     )
 
 
@@ -152,21 +198,38 @@
     samples = lax.axis_size("sample")
     imps = imp_user.shape[0]
     history = slots * sources * 2 // 3
+    like = lambda array: jax.ShapeDtypeStruct(array.shape, array.dtype)
+    row = lambda vector: vector.reshape(1, -1)
+    chips = sources // 2
+    sides = [[2 * chip + core for chip in range(chips)] for core in range(2)]
+    other_rows = lax.ppermute(table_rows, "table", [(i, i ^ 1) for i in range(sources)])
     with jax.named_scope("pack_ids"):
+        words = pack_words(jnp.transpose(hist_ids, (0, 2, 1)), hist_lens)
         words = kernel_call(
-            pack_kernel,
-            jax.ShapeDtypeStruct((sources, 1, users * slots // 2), jnp.int32),
-            1 << 20,
-        )(jnp.transpose(hist_ids, (0, 2, 1)), hist_lens)
-    words = lax.all_to_all(words, "table", split_axis=0, concat_axis=0, tiled=True)
+            turn_kernel,
+            jax.ShapeDtypeStruct((chips, 2, users * slots // 2), jnp.int32),
+            1 << 34,
+        )(words)
+    words = lax.all_to_all(
+        words, "table", split_axis=0, concat_axis=0, tiled=True, axis_index_groups=sides
+    )
+    vectors = tuple(map(row, (imp_user, labels, b_hidden, b_cross, norm_gain, w_score)))
     with jax.named_scope("pool"):
-        partials = kernel_call(
-            lambda *refs: pool_kernel(users, *refs),
-            jax.ShapeDtypeStruct((sources, users, width), BF16),
-            1 << 32,
-            [pltpu.VMEM((table_count // LOW, sources * users, LOW), BF16)],
-        )(words, table_rows)
-    returned = lax.all_to_all(partials, "table", split_axis=0, concat_axis=0, tiled=True)
+        partials, *vectors = kernel_call(
+            lambda *refs: pool_kernel(users, len(vectors), *refs),
+            (jax.ShapeDtypeStruct((chips, users, width), BF16),) + tuple(map(like, vectors)),
+            1 << 33,
+            in_specs=[VMEM, VMEM] + [HBM] * (1 + len(vectors)),
+            scratch=[
+                pltpu.VMEM((2 * (table_count // LOW), chips * users, LOW), BF16),
+                pltpu.VMEM((table_count, width), BF16),
+                pltpu.SemaphoreType.DMA((1 + len(vectors),)),
+            ],
+        )(words, other_rows, table_rows, *vectors)
+    imp_row, label_row, b_hidden, b_cross, norm_gain, w_score = vectors
+    returned = lax.all_to_all(
+        partials, "table", split_axis=0, concat_axis=0, tiled=True, axis_index_groups=sides
+    )
     pooled_user = (jnp.sum(returned.astype(F32), axis=0) * float(history) ** (-0.5)).astype(BF16)
     group_rows = lax.all_to_all(
         jnp.broadcast_to(pooled_user[None], (samples, users, width)),
@@ -175,7 +238,6 @@
         concat_axis=0,
         tiled=True,
     ).reshape(samples * users, width)
-    row = lambda vector: vector.reshape(1, -1)
     with jax.named_scope("dense"):
         scores, item_grad, per_user = kernel_call(
             dense_kernel,
@@ -187,21 +249,29 @@
             1 << 30,
         )(
             group_rows,
-            row(imp_user),
+            imp_row,
             item_rows,
-            row(labels),
+            label_row,
             w_hidden,
-            row(b_hidden),
+            b_hidden,
             w_back,
             w_cross,
-            row(b_cross),
-            row(norm_gain),
-            row(w_score),
+            b_cross,
+            norm_gain,
+            w_score,
         )
     parts = lax.all_to_all(
         per_user.reshape(samples, users, width), "sample", split_axis=0, concat_axis=0, tiled=True
     )
-    user_grad = jnp.sum(parts.astype(F32), axis=0)
+    with jax.named_scope("finish"):
+        user_grad, item_grad, scores, pooled_user = kernel_call(
+            finish_kernel,
+            (jax.ShapeDtypeStruct((users, width), F32), like(item_grad), like(scores), like(pooled_user)),
+            1 << 20,
+            in_specs=[VMEM] * 4,
+            out_specs=[HBM] * 4,
+            scratch=[pltpu.VMEM((users, width), F32), pltpu.SemaphoreType.DMA((4,))],
+        )(parts, item_grad, scores, pooled_user)
     return (pooled_user, scores.reshape(-1), user_grad, item_grad)
 
 

time: 117 us -> 97.9 us (0.84)
  blocking collectives: 94.1 us -> 84.4 us
  Pallas kernels: 17.2 us -> 8.54 us
  local copies, waits for them, and re-layouts: 4.16 us -> 0.71 us
  starting transfers between devices: 0 us -> 1.92 us
    pallas_call x2 -> x3, Pallas kernels: 14.7 us -> 6.54 us  [the longest x1 5.68 us: body(): kernel_call(lambda *refs: pool_kernel(users, len(vectors), *refs), (jax.S...]
    all_to_all x2, blocking collectives: 47.7 us -> 41.8 us  [the longest x1 25.9 us: body(): lax.all_to_all(words, 'table', split_axis=0, concat_axis=0, tiled=True, a...]
    unnamed x28 -> x22, local copies, waits for them, and re-layouts: 4.15 us -> 0.7 us
    all_to_all x1, blocking collectives: 19.7 us -> 16.9 us  [body(): lax.all_to_all(per_user.reshape(samples, users, width), 'sample', split_a...]
    ppermute x0 -> x1, starting transfers between devices: none -> 1.92 us  [body(): lax.ppermute(table_rows, 'table', [(i, i ^ 1) for i in range(sources)])]
  transfers between devices with their start and end apart: 0 -> 1, of which waited for: 0 -> 0; matrix products, arithmetic and copies ran while one was open for 0% -> 1% of each run, Pallas kernels for 0% -> 0%
where the time goes in v2:
time: 97.9 us; the launch traced here: 97.5 us
  blocking collectives  84.4 us (86%)
  Pallas kernels  8.54 us (9%)
  starting transfers between devices  1.92 us (2%)
  other arithmetic  1.11 us (1%)
    all_to_all x1, blocking collectives, body(): lax.all_to_all(words, 'table', split_axis=0, concat_axis=0, tiled=True, a...  25.9 us
    all_to_all x1, blocking collectives, body(): lax.all_to_all(jnp.broadcast_to(pooled_user[None], (samples, users, width...  25.8 us
    all_to_all x1, blocking collectives, body(): lax.all_to_all(per_user.reshape(samples, users, width), 'sample', split_a...  16.9 us
    all_to_all x1, blocking collectives, body(): lax.all_to_all(partials, 'table', split_axis=0, concat_axis=0, tiled=True...  15.9 us
    pallas_call x1, Pallas kernels, body(): kernel_call(lambda *refs: pool_kernel(users, len(vectors), *refs), (jax.S...  5.68 us
    pallas_call x1, Pallas kernels, body(): kernel_call(dense_kernel, (jax.ShapeDtypeStruct((1, imps), F32), jax.Shap...  2 us
  transfers between devices with their start and end apart: 1, of which 0 were waited for; matrix products, arithmetic and copies ran while one was open for 1% of the time, Pallas kernels for 0%

profile of v2, /device:TPU:8, one launch (start us, length us, event | category | flops | bytes accessed | tf_op | source)
XLA Modules:
  0.0 97.5 jit_solution(7441413198027763708)
XLA Ops:
  0.6 1.9 %collective-permute-start = (bf16[2048,256]{1,0:T(8,128)(2,1)}, bf16[2048,256]{1,0:T(8,128)(2,1)S(1)}, u32[]{:S(2)}, u32[]{:S(2)}) collective-permute-start(bf16[2048,256]{1,0:T(8,128)(2,1)} %refs_2_.1), channel_id=1, source_target_pairs={{0,16},{16,0},{32,48},{48,32},{64,80},{80,64},{96,112},{112,96},{1... | collective-permute-start | bytes 3145736 | tf_op jit(solution)/shard_map/ppermute | solution.py:205
  2.6 1.0 %bitcast_select_fusion = s32[16,48,64]{2,1,0:T(8,128)S(1)} fusion(s32[16,64,48]{1,2,0:T(8,128)} %param.13, s32[16,64]{1,0:T(8,128)} %param.14), kind=kLoop, calls=%fused_computation.1 | loop fusion | flops 98304 | bytes 397312 | tf_op jit(solution)/shard_map/pack_ids/jit(_where)/select_n | solution.py:21
  3.6 0.0 copy-start
  3.6 0.0 copy-start.6
  3.6 0.0 copy-start.7
  3.7 0.0 copy-start.8
  3.7 0.0 copy-start.10
  3.7 0.1 pack_ids.1
  3.8 25.9 %all_to_all.20.refs_0_ = s32[32,2,384]{2,1,0:T(2,128)S(1)} all-to-all(s32[32,2,384]{2,1,0:T(2,128)S(1)} %pack_ids.1), channel_id=1, replica_groups={{0,32,64,96,128,160,192,224,256,288,320,352,384,416,448,480,512,544,576..., dimensions={0} | all-to-all | bytes 196608 | tf_op jit(solution)/shard_map/all_to_all | solution.py:213
  29.7 0.0 collective-permute-done.refs_1_
  29.7 0.0 copy-start.5
  29.7 0.0 copy-start.9
  29.7 0.0 copy-done
  29.7 0.0 copy-done.6
  29.7 0.0 copy-done.7
  29.7 0.0 copy-done.8
  29.7 0.0 copy-done.10
  29.7 0.6 copy-done.5
  30.4 0.0 copy-done.9
  30.4 0.0 copy-start.3
  30.4 5.7 %pool.1 = (bf16[32,16,256]{2,1,0:T(8,128)(2,1)S(1)}, s32[1,256]{1,0:T(1,128)S(1)}, s32[1,256]{1,0:T(1,128)S(1)}, f32[1,512]{1,0:T(1,128)S(1)}, f32[1,512]{1,0:T(...) custom-call(s32[32,2,384]{2,1,0:T(2,128)S(1)} %all_to_all.20.refs_0_, ...), custom_call_target="tpu_custom_call" | custom-call | flops 8589934592 | bytes 2097152 | tf_op jit(solution)/shard_map/pool/pallas_call | solution.py:218
  36.1 0.0 copy-start.1
  36.1 0.0 copy-start.2
  36.1 15.9 %all_to_all.21 = bf16[32,16,256]{2,1,0:T(8,128)(2,1)S(1)} all-to-all(bf16[32,16,256]{2,1,0:T(8,128)(2,1)S(1)} %get-tuple-element.18), channel_id=1, replica_groups={{0,32,64,96,128,160,192,224,256,288,320,352,384,416,448,480,512,544,576..., dimensions={0} | all-to-all | bytes 524288 | tf_op jit(solution)/shard_map/all_to_all | solution.py:230
  52.1 0.0 copy-start.4
  52.1 25.8 %all_to_all.22 = bf16[16,16,256]{2,1,0:T(8,128)(2,1)S(1)} all-to-all(bf16[16,16,256]{2,1,0:T(8,128)(2,1)S(1)} %broadcast_in_dim.12), channel_id=1, replica_groups=mesh['table'=64,'sample'=16] {'sample'}, dimensions={0} | all-to-all | bytes 262144 | tf_op jit(solution)/shard_map/all_to_all | solution.py:234
  77.9 0.0 copy-done.3
  77.9 0.0 copy-done.1
  77.9 0.0 copy-done.2
  77.9 0.0 copy-done.4
  77.9 2.0 %dense.1 = (f32[1,256]{1,0:T(1,128)S(1)}, f32[256,256]{1,0:T(8,128)S(1)}, bf16[256,256]{1,0:T(8,128)(2,1)S(1)}) custom-call(bf16[256,256]{1,0:T(8,128)(2,1)S(1)} %bitcast.11, s32[1,256]{1,0:T(1,128)S(1)} %get-tuple-element.19.imp_ref, bf16[256,256]{1,0:T(8,128)(2,1)S(1)} %copy-done.4, s32[1,256]{1,0:T(1,128)S(1)} %get-tuple-element.20.labels_ref, ...), custom_call_target="tpu_custom_call" | custom-call | flops 1073741824 | bytes 2097152 | tf_op jit(solution)/shard_map/dense/pallas_call | solution.py:242
  79.9 16.9 %all_to_all.23.parts_ref = bf16[16,16,256]{2,1,0:T(8,128)(2,1)S(1)} all-to-all(bf16[16,16,256]{2,1,0:T(8,128)(2,1)S(1)} %bitcast.12), channel_id=1, replica_groups=mesh['table'=64,'sample'=16] {'sample'}, dimensions={0} | all-to-all | bytes 262144 | tf_op jit(solution)/shard_map/all_to_all | solution.py:263
  96.8 0.7 finish.1
  (4 shorter events, 0.1 us)
Async XLA Ops:
  0.6 29.1 %collective-permute-start = (bf16[2048,256]{1,0:T(8,128)(2,1)}, bf16[2048,256]{1,0:T(8,128)(2,1)S(1)}, u32[]{:S(2)}, u32[]{:S(2)}) collective-permute-start(bf16[2048,256]{1,0:T(8,128)(2,1)} %refs_2_.1), channel_id=1, source_target_pairs={{0,16},{16,0},{32,48},{48,32},{64,80},{80,64},{96,112},{112,96},{1... | collective-permute-start | bytes 3145736 | tf_op jit(solution)/shard_map/ppermute | solution.py:205
  3.6 26.1 %copy-start = (bf16[2048,256]{1,0:T(8,128)(2,1)S(1)}, bf16[2048,256]{1,0:T(8,128)(2,1)}, u32[]{:S(2)}) copy-start(bf16[2048,256]{1,0:T(8,128)(2,1)} %refs_2_.1) | copy-start | bytes 3145732
  3.6 26.1 %copy-start.6 = (f32[512]{0:T(512)S(1)}, f32[512]{0:T(512)}, u32[]{:S(2)}) copy-start(f32[512]{0:T(512)} %param.23) | copy-start | bytes 6148
  3.6 26.1 %copy-start.7 = (f32[512]{0:T(512)S(1)}, f32[512]{0:T(512)}, u32[]{:S(2)}) copy-start(f32[512]{0:T(512)} %param.24) | copy-start | bytes 6148
  3.7 26.1 %copy-start.8 = (f32[512]{0:T(512)S(1)}, f32[512]{0:T(512)}, u32[]{:S(2)}) copy-start(f32[512]{0:T(512)} %param.25) | copy-start | bytes 6148
  3.7 26.1 %copy-start.10 = (s32[256]{0:T(256)S(1)}, s32[256]{0:T(256)}, u32[]{:S(2)}) copy-start(s32[256]{0:T(256)} %param.18) | copy-start | bytes 3076
  29.7 0.7 copy-start.5
  29.7 0.7 copy-start.9
  30.4 47.5 %copy-start.3 = (bf16[512,512]{1,0:T(8,128)(2,1)S(1)}, bf16[512,512]{1,0:T(8,128)(2,1)}, u32[]{:S(2)}) copy-start(bf16[512,512]{1,0:T(8,128)(2,1)} %w_cross_ref.1) | copy-start | bytes 1572868
  36.1 41.8 %copy-start.1 = (bf16[512,512]{1,0:T(8,128)(2,1)S(1)}, bf16[512,512]{1,0:T(8,128)(2,1)}, u32[]{:S(2)}) copy-start(bf16[512,512]{1,0:T(8,128)(2,1)} %w_hidden_ref.1) | copy-start | bytes 1572868
  36.1 41.8 %copy-start.2 = (bf16[512,512]{1,0:T(8,128)(2,1)S(1)}, bf16[512,512]{1,0:T(8,128)(2,1)}, u32[]{:S(2)}) copy-start(bf16[512,512]{1,0:T(8,128)(2,1)} %w_back_ref.1) | copy-start | bytes 1572868
  52.1 25.8 %copy-start.4 = (bf16[256,256]{1,0:T(8,128)(2,1)S(1)}, bf16[256,256]{1,0:T(8,128)(2,1)}, u32[]{:S(2)}) copy-start(bf16[256,256]{1,0:T(8,128)(2,1)} %item_ref.1) | copy-start | bytes 393220

commit v3 on v2

--- a/solution.py
+++ b/solution.py
@@ -9,7 +9,7 @@
 BF16 = jnp.bfloat16
 F8 = jnp.float8_e4m3fn
 LOW = 256
-VMEM_LIMIT = 48 * 1024 * 1024
+VMEM_LIMIT = 32 * 1024 * 1024
 
 
 def rows_by_rows(a, b):
@@ -31,18 +31,14 @@
         out_ref[chip] = words[chip * cores : (chip + 1) * cores]
 
 
-def pool_kernel(users, n_staged, words_ref, other_ref, table_hbm, *refs):
-    staged_hbm, (out_ref, *staged_refs) = refs[:n_staged], refs[n_staged : 2 * n_staged + 1]
-    counts_ref, table_ref, sems = refs[2 * n_staged + 1 :]
-    copies = [pltpu.make_async_copy(table_hbm, table_ref, sems.at[0])]
-    for i, (source, target) in enumerate(zip(staged_hbm, staged_refs)):
-        copies.append(pltpu.make_async_copy(source, target, sems.at[i + 1]))
-    for copy in copies:
-        copy.start()
+def count_kernel(users, n_staged, words_ref, *refs):
+    staged, (counts_ref, *staged_refs) = refs[:n_staged], refs[n_staged:]
+    for source_ref, target_ref in zip(staged, staged_refs):
+        target_ref[...] = source_ref[...]
     sources = words_ref.shape[0]
     first_core = lax.rem(lax.axis_index("table"), 2) == 0
     positions = 2 * words_ref.shape[2]
-    highs = table_ref.shape[0] // LOW
+    highs = counts_ref.shape[0] // 2
     slots = positions // users
     user_of = lax.broadcasted_iota(jnp.int32, (1, positions), 1) // slots
     high_rows = lax.broadcasted_iota(jnp.int32, (highs * users, positions), 0).astype(jnp.int8)
@@ -66,22 +62,25 @@
                 counts_ref[shard * highs + part, rows, :] = counts[part * users : (part + 1) * users]
         return carry
 
-    lax.fori_loop(0, sources, count, 0, unroll=8)
-    for copy in copies:
-        copy.wait()
+    lax.fori_loop(0, sources, count, 0, unroll=32)
+
+
+def pool_kernel(counts_ref, own_ref, other_ref, out_ref):
+    parts = counts_ref.shape[0]
+    sources, users, width = out_ref.shape
     chunk = 16
     for first in range(0, sources, chunk):
         total = None
-        for part in range(2 * highs):
-            shard_ref = (table_ref, other_ref)[part // highs]
-            low_row = part % highs * LOW
+        for part in range(parts):
+            shard_ref = (own_ref, other_ref)[part // (parts // 2)]
+            low_row = part % (parts // 2) * LOW
             term = jnp.dot(
                 counts_ref[part, first * users : (first + chunk) * users, :],
                 shard_ref[low_row : low_row + LOW, :],
                 preferred_element_type=F32,
             )
             total = term if total is None else total + term
-        out_ref[first : first + chunk] = total.astype(BF16).reshape(chunk, users, total.shape[1])
+        out_ref[first : first + chunk] = total.astype(BF16).reshape(chunk, users, width)
 
 
 def dense_kernel(
@@ -202,7 +201,6 @@
     row = lambda vector: vector.reshape(1, -1)
     chips = sources // 2
     sides = [[2 * chip + core for chip in range(chips)] for core in range(2)]
-    other_rows = lax.ppermute(table_rows, "table", [(i, i ^ 1) for i in range(sources)])
     with jax.named_scope("pack_ids"):
         words = pack_words(jnp.transpose(hist_ids, (0, 2, 1)), hist_lens)
         words = kernel_call(
@@ -210,22 +208,22 @@
             jax.ShapeDtypeStruct((chips, 2, users * slots // 2), jnp.int32),
             1 << 34,
         )(words)
+    other_rows = lax.ppermute(table_rows, "table", [(i, i ^ 1) for i in range(sources)])
     words = lax.all_to_all(
         words, "table", split_axis=0, concat_axis=0, tiled=True, axis_index_groups=sides
     )
     vectors = tuple(map(row, (imp_user, labels, b_hidden, b_cross, norm_gain, w_score)))
+    with jax.named_scope("count"):
+        counts, *vectors = kernel_call(
+            lambda *refs: count_kernel(users, len(vectors), *refs),
+            (jax.ShapeDtypeStruct((2 * (table_count // LOW), chips * users, LOW), BF16),)
+            + tuple(map(like, vectors)),
+            1 << 33,
+        )(words, *vectors)
     with jax.named_scope("pool"):
-        partials, *vectors = kernel_call(
-            lambda *refs: pool_kernel(users, len(vectors), *refs),
-            (jax.ShapeDtypeStruct((chips, users, width), BF16),) + tuple(map(like, vectors)),
-            1 << 33,
-            in_specs=[VMEM, VMEM] + [HBM] * (1 + len(vectors)),
-            scratch=[
-                pltpu.VMEM((2 * (table_count // LOW), chips * users, LOW), BF16),
-                pltpu.VMEM((table_count, width), BF16),
-                pltpu.SemaphoreType.DMA((1 + len(vectors),)),
-            ],
-        )(words, other_rows, table_rows, *vectors)
+        partials = kernel_call(
+            pool_kernel, jax.ShapeDtypeStruct((chips, users, width), BF16), 1 << 30
+        )(counts, table_rows, other_rows)
     imp_row, label_row, b_hidden, b_cross, norm_gain, w_score = vectors
     returned = lax.all_to_all(
         partials, "table", split_axis=0, concat_axis=0, tiled=True, axis_index_groups=sides

time: 97.9 us -> 96.1 us (0.982)
    pallas_call x1 -> x2, Pallas kernels: 5.68 us -> 4.98 us  [the longest x1 3.73 us: body(): kernel_call(lambda *refs: count_kernel(users, len(vectors), *refs), (jax....]
  transfers between devices with their start and end apart: 1 -> 1, of which waited for: 0 -> 0; matrix products, arithmetic and copies ran while one was open for 1% -> 1% of each run, Pallas kernels for 0% -> 4%
where the time goes in v3:
time: 96.1 us; the launch traced here: 95.8 us
  blocking collectives  84 us (87%)
  Pallas kernels  7.84 us (8%)
  starting transfers between devices  1.92 us (2%)
  other arithmetic  1.11 us (1%)
    all_to_all x1, blocking collectives, body(): lax.all_to_all(words, 'table', split_axis=0, concat_axis=0, tiled=True, a...  25.7 us
    all_to_all x1, blocking collectives, body(): lax.all_to_all(jnp.broadcast_to(pooled_user[None], (samples, users, width...  25.7 us
    all_to_all x1, blocking collectives, body(): lax.all_to_all(per_user.reshape(samples, users, width), 'sample', split_a...  16.9 us
    all_to_all x1, blocking collectives, body(): lax.all_to_all(partials, 'table', split_axis=0, concat_axis=0, tiled=True...  15.8 us
    pallas_call x1, Pallas kernels, body(): kernel_call(lambda *refs: count_kernel(users, len(vectors), *refs), (jax....  3.73 us
    pallas_call x1, Pallas kernels, body(): kernel_call(dense_kernel, (jax.ShapeDtypeStruct((1, imps), F32), jax.Shap...  2 us
    ppermute x1, starting transfers between devices, body(): lax.ppermute(table_rows, 'table', [(i, i ^ 1) for i in range(sources)])  1.92 us
  transfers between devices with their start and end apart: 1, of which 0 were waited for; matrix products, arithmetic and copies ran while one was open for 1% of the time, Pallas kernels for 4%

profile of v3, /device:TPU:8, one launch (start us, length us, event | category | flops | bytes accessed | tf_op | source)
XLA Modules:
  0.0 95.8 jit_solution(2513841208713235380)
XLA Ops:
  0.6 1.9 %collective-permute-start = (bf16[2048,256]{1,0:T(8,128)(2,1)}, bf16[2048,256]{1,0:T(8,128)(2,1)S(1)}, u32[]{:S(2)}, u32[]{:S(2)}) collective-permute-start(bf16[2048,256]{1,0:T(8,128)(2,1)} %own_ref.1), channel_id=1, source_target_pairs={{0,16},{16,0},{32,48},{48,32},{64,80},{80,64},{96,112},{112,96},{1... | collective-permute-start | bytes 3145736 | tf_op jit(solution)/shard_map/ppermute | solution.py:211
  2.6 1.0 %bitcast_select_fusion = s32[16,48,64]{2,1,0:T(8,128)S(1)} fusion(s32[16,64,48]{1,2,0:T(8,128)} %param.13, s32[16,64]{1,0:T(8,128)} %param.14), kind=kLoop, calls=%fused_computation.1 | loop fusion | flops 98304 | bytes 397312 | tf_op jit(solution)/shard_map/pack_ids/jit(_where)/select_n | solution.py:21
  3.6 0.0 copy-start.5
  3.6 0.0 copy-start.6
  3.6 0.0 copy-start.7
  3.7 0.0 copy-start.8
  3.7 0.0 copy-start.9
  3.7 0.0 copy-start.10
  3.7 0.1 pack_ids.1
  3.8 25.7 %all_to_all.20.refs_0_ = s32[32,2,384]{2,1,0:T(2,128)S(1)} all-to-all(s32[32,2,384]{2,1,0:T(2,128)S(1)} %pack_ids.1), channel_id=1, replica_groups={{0,32,64,96,128,160,192,224,256,288,320,352,384,416,448,480,512,544,576..., dimensions={0} | all-to-all | bytes 196608 | tf_op jit(solution)/shard_map/all_to_all | solution.py:212
  29.6 0.0 copy-done.5
  29.6 0.0 copy-done.6
  29.6 0.0 copy-done.7
  29.6 0.0 copy-done.8
  29.6 0.0 copy-done.9
  29.6 0.0 copy-done.10
  29.6 0.0 copy-start
  29.6 3.7 %count.1 = (bf16[16,512,256]{2,1,0:T(8,128)(2,1)S(1)}, s32[1,256]{1,0:T(1,128)S(1)}, s32[1,256]{1,0:T(1,128)S(1)}, f32[1,512]{1,0:T(1,128)S(1)}, f32[1,512]{1,0:...) custom-call(s32[32,2,384]{2,1,0:T(2,128)S(1)} %all_to_all.20.refs_0_, s32[1,256]{1,0:T(1,128)S(1)} %bitcast.17, ...), custom_call_target="tpu_custom_call" | custom-call | flops 8589934592 | bytes 2097152 | tf_op jit(solution)/shard_map/count/pallas_call | solution.py:217
  33.4 0.0 copy-start.1
  33.4 0.0 copy-start.2
  33.4 0.0 copy-start.3
  33.4 0.0 copy-start.4
  33.4 0.0 collective-permute-done.other_ref
  33.4 0.0 copy-done
  33.4 1.2 %pool.1 = bf16[32,16,256]{2,1,0:T(8,128)(2,1)S(1)} custom-call(bf16[16,512,256]{2,1,0:T(8,128)(2,1)S(1)} %get-tuple-element.18.counts_ref, bf16[2048,256]{1,0:T(8,128)(2,1)S(1)} %copy-done, bf16[2048,256]{1,0:T(8,128)(2,1)S(1)} %collective-permute-done.other_ref), custom_call_target="tpu_custom_call" | custom-call | flops 1073741824 | bytes 2097152 | tf_op jit(solution)/shard_map/pool/pallas_call | solution.py:224
  34.7 15.8 %all_to_all.21 = bf16[32,16,256]{2,1,0:T(8,128)(2,1)S(1)} all-to-all(bf16[32,16,256]{2,1,0:T(8,128)(2,1)S(1)} %pool.1), channel_id=1, replica_groups={{0,32,64,96,128,160,192,224,256,288,320,352,384,416,448,480,512,544,576..., dimensions={0} | all-to-all | bytes 524288 | tf_op jit(solution)/shard_map/all_to_all | solution.py:228
  50.5 25.7 %all_to_all.22 = bf16[16,16,256]{2,1,0:T(8,128)(2,1)S(1)} all-to-all(bf16[16,16,256]{2,1,0:T(8,128)(2,1)S(1)} %broadcast_in_dim.12), channel_id=1, replica_groups=mesh['table'=64,'sample'=16] {'sample'}, dimensions={0} | all-to-all | bytes 262144 | tf_op jit(solution)/shard_map/all_to_all | solution.py:232
  76.2 0.0 copy-done.1
  76.2 0.0 copy-done.2
  76.2 0.0 copy-done.3
  76.2 0.0 copy-done.4
  76.2 2.0 %dense.1 = (f32[1,256]{1,0:T(1,128)S(1)}, f32[256,256]{1,0:T(8,128)S(1)}, bf16[256,256]{1,0:T(8,128)(2,1)S(1)}) custom-call(bf16[256,256]{1,0:T(8,128)(2,1)S(1)} %bitcast.11, s32[1,256]{1,0:T(1,128)S(1)} %get-tuple-element.19.imp_ref, bf16[256,256]{1,0:T(8,128)(2,1)S(1)} %copy-done.4, s32[1,256]{1,0:T(1,128)S(1)} %get-tuple-element.20.labels_ref, ...), custom_call_target="tpu_custom_call" | custom-call | flops 1073741824 | bytes 2097152 | tf_op jit(solution)/shard_map/dense/pallas_call | solution.py:240
  78.2 16.9 %all_to_all.23.parts_ref = bf16[16,16,256]{2,1,0:T(8,128)(2,1)S(1)} all-to-all(bf16[16,16,256]{2,1,0:T(8,128)(2,1)S(1)} %bitcast.12), channel_id=1, replica_groups=mesh['table'=64,'sample'=16] {'sample'}, dimensions={0} | all-to-all | bytes 262144 | tf_op jit(solution)/shard_map/all_to_all | solution.py:261
  95.1 0.7 finish.1
  (4 shorter events, 0.1 us)
Async XLA Ops:
  0.6 32.8 %collective-permute-start = (bf16[2048,256]{1,0:T(8,128)(2,1)}, bf16[2048,256]{1,0:T(8,128)(2,1)S(1)}, u32[]{:S(2)}, u32[]{:S(2)}) collective-permute-start(bf16[2048,256]{1,0:T(8,128)(2,1)} %own_ref.1), channel_id=1, source_target_pairs={{0,16},{16,0},{32,48},{48,32},{64,80},{80,64},{96,112},{112,96},{1... | collective-permute-start | bytes 3145736 | tf_op jit(solution)/shard_map/ppermute | solution.py:211
  3.6 25.9 %copy-start.5 = (f32[512]{0:T(512)S(1)}, f32[512]{0:T(512)}, u32[]{:S(2)}) copy-start(f32[512]{0:T(512)} %param.20) | copy-start | bytes 6148
  3.6 25.9 %copy-start.6 = (f32[512]{0:T(512)S(1)}, f32[512]{0:T(512)}, u32[]{:S(2)}) copy-start(f32[512]{0:T(512)} %param.23) | copy-start | bytes 6148
  3.6 25.9 %copy-start.7 = (f32[512]{0:T(512)S(1)}, f32[512]{0:T(512)}, u32[]{:S(2)}) copy-start(f32[512]{0:T(512)} %param.24) | copy-start | bytes 6148
  3.7 25.9 %copy-start.8 = (f32[512]{0:T(512)S(1)}, f32[512]{0:T(512)}, u32[]{:S(2)}) copy-start(f32[512]{0:T(512)} %param.25) | copy-start | bytes 6148
  3.7 25.9 %copy-start.9 = (s32[256]{0:T(256)S(1)}, s32[256]{0:T(256)}, u32[]{:S(2)}) copy-start(s32[256]{0:T(256)} %param.16) | copy-start | bytes 3076
  3.7 25.9 %copy-start.10 = (s32[256]{0:T(256)S(1)}, s32[256]{0:T(256)}, u32[]{:S(2)}) copy-start(s32[256]{0:T(256)} %param.18) | copy-start | bytes 3076
  29.6 3.8 %copy-start = (bf16[2048,256]{1,0:T(8,128)(2,1)S(1)}, bf16[2048,256]{1,0:T(8,128)(2,1)}, u32[]{:S(2)}) copy-start(bf16[2048,256]{1,0:T(8,128)(2,1)} %own_ref.1) | copy-start | bytes 3145732
  33.4 42.9 %copy-start.1 = (bf16[512,512]{1,0:T(8,128)(2,1)S(1)}, bf16[512,512]{1,0:T(8,128)(2,1)}, u32[]{:S(2)}) copy-start(bf16[512,512]{1,0:T(8,128)(2,1)} %w_hidden_ref.1) | copy-start | bytes 1572868
  33.4 42.8 %copy-start.2 = (bf16[512,512]{1,0:T(8,128)(2,1)S(1)}, bf16[512,512]{1,0:T(8,128)(2,1)}, u32[]{:S(2)}) copy-start(bf16[512,512]{1,0:T(8,128)(2,1)} %w_back_ref.1) | copy-start | bytes 1572868
  33.4 42.8 %copy-start.3 = (bf16[512,512]{1,0:T(8,128)(2,1)S(1)}, bf16[512,512]{1,0:T(8,128)(2,1)}, u32[]{:S(2)}) copy-start(bf16[512,512]{1,0:T(8,128)(2,1)} %w_cross_ref.1) | copy-start | bytes 1572868
  33.4 42.8 %copy-start.4 = (bf16[256,256]{1,0:T(8,128)(2,1)S(1)}, bf16[256,256]{1,0:T(8,128)(2,1)}, u32[]{:S(2)}) copy-start(bf16[256,256]{1,0:T(8,128)(2,1)} %item_ref.1) | copy-start | bytes 393220

commit v4 on v3

--- a/solution.py
+++ b/solution.py
@@ -8,7 +8,10 @@
 F32 = jnp.float32
 BF16 = jnp.bfloat16
 F8 = jnp.float8_e4m3fn
-LOW = 256
+LOW_BITS = 7
+LOW = 1 << LOW_BITS
+DEPTH = 256
+HALF = 8
 VMEM_LIMIT = 32 * 1024 * 1024
 
 
@@ -31,52 +34,67 @@
         out_ref[chip] = words[chip * cores : (chip + 1) * cores]
 
 
-def count_kernel(users, n_staged, words_ref, *refs):
-    staged, (counts_ref, *staged_refs) = refs[:n_staged], refs[n_staged:]
-    for source_ref, target_ref in zip(staged, staged_refs):
-        target_ref[...] = source_ref[...]
+def count_kernel(users, words_ref, *refs):
+    counts_ref = refs[-1]
     sources = words_ref.shape[0]
     first_core = lax.rem(lax.axis_index("table"), 2) == 0
     positions = 2 * words_ref.shape[2]
-    highs = counts_ref.shape[0] // 2
     slots = positions // users
-    user_of = lax.broadcasted_iota(jnp.int32, (1, positions), 1) // slots
-    high_rows = lax.broadcasted_iota(jnp.int32, (highs * users, positions), 0).astype(jnp.int8)
-    low_rows = (lax.broadcasted_iota(jnp.int32, (LOW, positions), 0) - LOW // 2).astype(jnp.int8)
+    side_by_side = counts_ref.shape[2] // LOW
+    highs = counts_ref.shape[0] // 2 * side_by_side
+    low_rows = lax.broadcasted_iota(jnp.int32, (LOW, positions), 0).astype(jnp.int8)
     one, zero = jnp.ones((), F8), jnp.zeros((), F8)
+    tiles = []
+    for first in range(0, positions, DEPTH):
+        groups = sorted({first // slots // HALF, (first + DEPTH - 1) // slots // HALF})
+        rows = len(groups) * HALF
+        middle = highs * rows // 2
+        user = (lax.broadcasted_iota(jnp.int32, (1, DEPTH), 1) + first) // slots - groups[0] * HALF
+        code_rows = lax.broadcasted_iota(jnp.int32, (highs * rows, DEPTH), 0) - middle
+        tiles.append((slice(first, first + DEPTH), groups, rows, user - middle, code_rows.astype(jnp.int8)))
 
     def count(source, carry):
         pair = words_ref[source]
         own = jnp.where(first_core, pair[:1], pair[1:])
         other = jnp.where(first_core, pair[1:], pair[:1])
-        rows = pl.ds(pl.multiple_of(source * users, users), users)
+        target = pl.ds(pl.multiple_of(source * users, users), users)
         for shard, words in enumerate((own, other)):
             ids = jnp.concatenate([words & 0xFFFF, (words >> 16) & 0xFFFF], axis=1)
-            high = (ids // LOW) * users + user_of
-            high = jnp.where(high < highs * users, high, -1).astype(jnp.int8)
-            low = (ids % LOW - LOW // 2).astype(jnp.int8)
-            high_hot = jnp.where(high == high_rows, one, zero)
+            low = jnp.where(ids < highs * LOW, ids & (LOW - 1), -1).astype(jnp.int8)
+            high = (ids >> LOW_BITS) & (highs - 1)
             low_hot = jnp.where(low == low_rows, one, zero)
-            counts = rows_by_rows(high_hot, low_hot).astype(BF16)
+            found = {}
+            for piece, groups, rows, base, code_rows in tiles:
+                code = (high[:, piece] * rows + base).astype(jnp.int8)
+                high_hot = jnp.where(code == code_rows, one, zero)
+                counts = rows_by_rows(high_hot, low_hot[:, piece])
+                for part in range(highs):
+                    for i, group in enumerate(groups):
+                        start = part * rows + i * HALF
+                        found.setdefault((part, group), []).append(counts[start : start + HALF])
             for part in range(highs):
-                counts_ref[shard * highs + part, rows, :] = counts[part * users : (part + 1) * users]
+                sums = [sum(found[part, group][1:], found[part, group][0]) for group in range(users // HALF)]
+                lane = part % side_by_side * LOW
+                counts_ref[(shard * highs + part) // side_by_side, target, lane : lane + LOW] = jnp.concatenate(
+                    sums, axis=0
+                ).astype(BF16)
         return carry
 
     lax.fori_loop(0, sources, count, 0, unroll=32)
 
 
 def pool_kernel(counts_ref, own_ref, other_ref, out_ref):
-    parts = counts_ref.shape[0]
+    parts, _, depth = counts_ref.shape
     sources, users, width = out_ref.shape
     chunk = 16
     for first in range(0, sources, chunk):
         total = None
         for part in range(parts):
             shard_ref = (own_ref, other_ref)[part // (parts // 2)]
-            low_row = part % (parts // 2) * LOW
+            low_row = part % (parts // 2) * depth
             term = jnp.dot(
                 counts_ref[part, first * users : (first + chunk) * users, :],
-                shard_ref[low_row : low_row + LOW, :],
+                shard_ref[low_row : low_row + depth, :],
                 preferred_element_type=F32,
             )
             total = term if total is None else total + term
@@ -110,14 +128,14 @@
     joined = jnp.concatenate([user_feat, item_ref[...]], axis=1)
     lifted = joined.astype(F32)
     pre = jnp.dot(joined, w_hidden_ref[...], preferred_element_type=F32) + b_hidden_ref[...]
-    cross = jnp.dot(joined, w_cross_ref[...], preferred_element_type=F32) + b_cross_ref[...]
+    factor = jnp.dot(joined, w_cross_ref[...], preferred_element_type=F32) + (b_cross_ref[...] + 1.0)
     k, c = 0.7978845608028654, 0.044715
     square = pre * pre
-    tanh = jnp.tanh(k * pre * (1.0 + c * square))
-    cdf = 0.5 * (1.0 + tanh)
+    half_tanh = 0.5 * jnp.tanh(pre * (k + (k * c) * square))
+    cdf = 0.5 + half_tanh
     hidden = (pre * cdf).astype(BF16)
-    slope = cdf + 0.5 * pre * (1.0 - tanh * tanh) * (k * (1.0 + 3.0 * c * square))
-    summed = lifted + jnp.dot(hidden, w_back_ref[...], preferred_element_type=F32) + lifted * cross
+    slope = cdf + (cdf * (0.5 - half_tanh)) * (pre * (2.0 * k + (6.0 * k * c) * square))
+    summed = jnp.dot(hidden, w_back_ref[...], preferred_element_type=F32) + lifted * factor
     columns = summed.shape[1]
     centred = summed - jnp.sum(summed, axis=1, keepdims=True) * (1.0 / columns)
     variance = jnp.sum(centred * centred, axis=1, keepdims=True) * (1.0 / columns)
@@ -133,7 +151,7 @@
     pre_grad = (hidden_grad * slope).astype(BF16)
     cross_grad = (summed_grad * lifted).astype(BF16)
     joined_grad = (
-        summed_grad * (1.0 + cross)
+        summed_grad * factor
         + rows_by_rows(pre_grad, w_hidden_ref[...])
         + rows_by_rows(cross_grad, w_cross_ref[...])
     )
@@ -214,10 +232,9 @@
     )
     vectors = tuple(map(row, (imp_user, labels, b_hidden, b_cross, norm_gain, w_score)))
     with jax.named_scope("count"):
-        counts, *vectors = kernel_call(
-            lambda *refs: count_kernel(users, len(vectors), *refs),
-            (jax.ShapeDtypeStruct((2 * (table_count // LOW), chips * users, LOW), BF16),)
-            + tuple(map(like, vectors)),
+        counts = kernel_call(
+            lambda *refs: count_kernel(users, *refs),
+            jax.ShapeDtypeStruct((2 * (table_count // DEPTH), chips * users, DEPTH), BF16),
             1 << 33,
         )(words, *vectors)
     with jax.named_scope("pool"):

time: 96.1 us -> 95.1 us (0.990)
  Pallas kernels: 7.84 us -> 6.8 us
    pallas_call x1, Pallas kernels: 3.73 us -> 2.67 us  [body(): kernel_call(lambda *refs: count_kernel(users, *refs), jax.ShapeDtypeStruc...]
  transfers between devices with their start and end apart: 1 -> 1, of which waited for: 0 -> 0; matrix products, arithmetic and copies ran while one was open for 1% -> 1% of each run, Pallas kernels for 4% -> 3%
where the time goes in v4:
time: 95.1 us; the launch traced here: 94.8 us
  blocking collectives  84 us (88%)
  Pallas kernels  6.8 us (7%)
  starting transfers between devices  1.92 us (2%)
  other arithmetic  1.11 us (1%)
    all_to_all x1, blocking collectives, body(): lax.all_to_all(words, 'table', split_axis=0, concat_axis=0, tiled=True, a...  25.7 us
    all_to_all x1, blocking collectives, body(): lax.all_to_all(jnp.broadcast_to(pooled_user[None], (samples, users, width...  25.7 us
    all_to_all x1, blocking collectives, body(): lax.all_to_all(per_user.reshape(samples, users, width), 'sample', split_a...  16.9 us
    all_to_all x1, blocking collectives, body(): lax.all_to_all(partials, 'table', split_axis=0, concat_axis=0, tiled=True...  15.8 us
    pallas_call x1, Pallas kernels, body(): kernel_call(lambda *refs: count_kernel(users, *refs), jax.ShapeDtypeStruc...  2.67 us
    pallas_call x1, Pallas kernels, body(): kernel_call(dense_kernel, (jax.ShapeDtypeStruct((1, imps), F32), jax.Shap...  2.02 us
    ppermute x1, starting transfers between devices, body(): lax.ppermute(table_rows, 'table', [(i, i ^ 1) for i in range(sources)])  1.92 us
  transfers between devices with their start and end apart: 1, of which 0 were waited for; matrix products, arithmetic and copies ran while one was open for 1% of the time, Pallas kernels for 3%

profile of v4, /device:TPU:8, one launch (start us, length us, event | category | flops | bytes accessed | tf_op | source)
XLA Modules:
  0.0 94.8 jit_solution(11871826798475186765)
XLA Ops:
  0.6 1.9 %collective-permute-start = (bf16[2048,256]{1,0:T(8,128)(2,1)}, bf16[2048,256]{1,0:T(8,128)(2,1)S(1)}, u32[]{:S(2)}, u32[]{:S(2)}) collective-permute-start(bf16[2048,256]{1,0:T(8,128)(2,1)} %own_ref.1), channel_id=1, source_target_pairs={{0,16},{16,0},{32,48},{48,32},{64,80},{80,64},{96,112},{112,96},{1... | collective-permute-start | bytes 3145736 | tf_op jit(solution)/shard_map/ppermute | solution.py:229
  2.6 1.0 %bitcast_select_fusion = s32[16,48,64]{2,1,0:T(8,128)S(1)} fusion(s32[16,64,48]{1,2,0:T(8,128)} %param.13, s32[16,64]{1,0:T(8,128)} %param.14), kind=kLoop, calls=%fused_computation.1 | loop fusion | flops 98304 | bytes 397312 | tf_op jit(solution)/shard_map/pack_ids/jit(_where)/select_n | solution.py:24
  3.6 0.0 copy-start.5
  3.6 0.0 copy-start.6
  3.6 0.0 copy-start.7
  3.7 0.0 copy-start.8
  3.7 0.0 copy-start.9
  3.7 0.0 copy-start.10
  3.7 0.1 pack_ids.1
  3.8 25.7 %all_to_all.20.refs_0_ = s32[32,2,384]{2,1,0:T(2,128)S(1)} all-to-all(s32[32,2,384]{2,1,0:T(2,128)S(1)} %pack_ids.1), channel_id=1, replica_groups={{0,32,64,96,128,160,192,224,256,288,320,352,384,416,448,480,512,544,576..., dimensions={0} | all-to-all | bytes 196608 | tf_op jit(solution)/shard_map/all_to_all | solution.py:230
  29.6 0.0 copy-done.5
  29.6 0.0 copy-done.6
  29.6 0.0 copy-done.7
  29.6 0.0 copy-done.8
  29.6 0.0 copy-done.9
  29.6 0.0 copy-done.10
  29.6 0.0 copy-start
  29.6 2.7 %count.1.counts_ref = bf16[16,512,256]{2,1,0:T(8,128)(2,1)S(1)} custom-call(s32[32,2,384]{2,1,0:T(2,128)S(1)} %all_to_all.20.refs_0_, s32[1,256]{1,0:T(1,128)S(1)} %bitcast.21, s32[1,256]{1,0:T(1,128)S(1)} %bitcast.23, f32[1,512]{1,0:T(1,128)S(1)} %bitcast.13, f32[1,512]{1,0:T(1,128)S(1)} %bitcast.15, f32[1,512]{1,0:T(1,128)S(1)} %bitcast.17, ...), custom_call_target="tpu_custom_call" | custom-call | flops 8589934592 | bytes 2097152 | tf_op jit(solution)/shard_map/count/pallas_call | solution.py:235
  32.3 0.0 copy-start.1
  32.3 0.0 copy-start.2
  32.3 0.0 copy-start.3
  32.3 0.0 copy-start.4
  32.3 0.0 collective-permute-done.other_ref
  32.4 0.0 copy-done
  32.4 1.2 %pool.1 = bf16[32,16,256]{2,1,0:T(8,128)(2,1)S(1)} custom-call(bf16[16,512,256]{2,1,0:T(8,128)(2,1)S(1)} %count.1.counts_ref, bf16[2048,256]{1,0:T(8,128)(2,1)S(1)} %copy-done, bf16[2048,256]{1,0:T(8,128)(2,1)S(1)} %collective-permute-done.other_ref), custom_call_target="tpu_custom_call" | custom-call | flops 1073741824 | bytes 2097152 | tf_op jit(solution)/shard_map/pool/pallas_call | solution.py:241
  33.6 15.8 %all_to_all.21 = bf16[32,16,256]{2,1,0:T(8,128)(2,1)S(1)} all-to-all(bf16[32,16,256]{2,1,0:T(8,128)(2,1)S(1)} %pool.1), channel_id=1, replica_groups={{0,32,64,96,128,160,192,224,256,288,320,352,384,416,448,480,512,544,576..., dimensions={0} | all-to-all | bytes 524288 | tf_op jit(solution)/shard_map/all_to_all | solution.py:245
  49.5 25.7 %all_to_all.22 = bf16[16,16,256]{2,1,0:T(8,128)(2,1)S(1)} all-to-all(bf16[16,16,256]{2,1,0:T(8,128)(2,1)S(1)} %broadcast_in_dim.12), channel_id=1, replica_groups=mesh['table'=64,'sample'=16] {'sample'}, dimensions={0} | all-to-all | bytes 262144 | tf_op jit(solution)/shard_map/all_to_all | solution.py:249
  75.1 0.0 copy-done.1
  75.1 0.0 copy-done.2
  75.1 0.0 copy-done.3
  75.2 0.0 copy-done.4
  75.2 2.0 %dense.1 = (f32[1,256]{1,0:T(1,128)S(1)}, f32[256,256]{1,0:T(8,128)S(1)}, bf16[256,256]{1,0:T(8,128)(2,1)S(1)}) custom-call(bf16[256,256]{1,0:T(8,128)(2,1)S(1)} %bitcast.11, s32[1,256]{1,0:T(1,128)S(1)} %bitcast.22, bf16[256,256]{1,0:T(8,128)(2,1)S(1)} %copy-done.4, s32[1,256]{1,0:T(1,128)S(1)} %bitcast.24, bf16[512,512]{1,0:T(8,128)(2,1)S(1)} %copy-done.1, ...), custom_call_target="tpu_custom_call" | custom-call | flops 1073741824 | bytes 2097152 | tf_op jit(solution)/shard_map/dense/pallas_call | solution.py:257
  77.2 16.9 %all_to_all.23.parts_ref = bf16[16,16,256]{2,1,0:T(8,128)(2,1)S(1)} all-to-all(bf16[16,16,256]{2,1,0:T(8,128)(2,1)S(1)} %bitcast.12), channel_id=1, replica_groups=mesh['table'=64,'sample'=16] {'sample'}, dimensions={0} | all-to-all | bytes 262144 | tf_op jit(solution)/shard_map/all_to_all | solution.py:278
  94.1 0.7 finish.1
  (4 shorter events, 0.1 us)
Async XLA Ops:
  0.6 31.7 %collective-permute-start = (bf16[2048,256]{1,0:T(8,128)(2,1)}, bf16[2048,256]{1,0:T(8,128)(2,1)S(1)}, u32[]{:S(2)}, u32[]{:S(2)}) collective-permute-start(bf16[2048,256]{1,0:T(8,128)(2,1)} %own_ref.1), channel_id=1, source_target_pairs={{0,16},{16,0},{32,48},{48,32},{64,80},{80,64},{96,112},{112,96},{1... | collective-permute-start | bytes 3145736 | tf_op jit(solution)/shard_map/ppermute | solution.py:229
  3.6 25.9 %copy-start.5 = (f32[512]{0:T(512)S(1)}, f32[512]{0:T(512)}, u32[]{:S(2)}) copy-start(f32[512]{0:T(512)} %param.20) | copy-start | bytes 6148
  3.6 25.9 %copy-start.6 = (f32[512]{0:T(512)S(1)}, f32[512]{0:T(512)}, u32[]{:S(2)}) copy-start(f32[512]{0:T(512)} %param.23) | copy-start | bytes 6148
  3.6 25.9 %copy-start.7 = (f32[512]{0:T(512)S(1)}, f32[512]{0:T(512)}, u32[]{:S(2)}) copy-start(f32[512]{0:T(512)} %param.24) | copy-start | bytes 6148
  3.7 25.9 %copy-start.8 = (f32[512]{0:T(512)S(1)}, f32[512]{0:T(512)}, u32[]{:S(2)}) copy-start(f32[512]{0:T(512)} %param.25) | copy-start | bytes 6148
  3.7 25.9 %copy-start.9 = (s32[256]{0:T(256)S(1)}, s32[256]{0:T(256)}, u32[]{:S(2)}) copy-start(s32[256]{0:T(256)} %param.16) | copy-start | bytes 3076
  3.7 25.9 %copy-start.10 = (s32[256]{0:T(256)S(1)}, s32[256]{0:T(256)}, u32[]{:S(2)}) copy-start(s32[256]{0:T(256)} %param.18) | copy-start | bytes 3076
  29.6 2.7 %copy-start = (bf16[2048,256]{1,0:T(8,128)(2,1)S(1)}, bf16[2048,256]{1,0:T(8,128)(2,1)}, u32[]{:S(2)}) copy-start(bf16[2048,256]{1,0:T(8,128)(2,1)} %own_ref.1) | copy-start | bytes 3145732
  32.3 42.9 %copy-start.1 = (bf16[512,512]{1,0:T(8,128)(2,1)S(1)}, bf16[512,512]{1,0:T(8,128)(2,1)}, u32[]{:S(2)}) copy-start(bf16[512,512]{1,0:T(8,128)(2,1)} %w_hidden_ref.1) | copy-start | bytes 1572868
  32.3 42.8 %copy-start.2 = (bf16[512,512]{1,0:T(8,128)(2,1)S(1)}, bf16[512,512]{1,0:T(8,128)(2,1)}, u32[]{:S(2)}) copy-start(bf16[512,512]{1,0:T(8,128)(2,1)} %w_back_ref.1) | copy-start | bytes 1572868
  32.3 42.8 %copy-start.3 = (bf16[512,512]{1,0:T(8,128)(2,1)S(1)}, bf16[512,512]{1,0:T(8,128)(2,1)}, u32[]{:S(2)}) copy-start(bf16[512,512]{1,0:T(8,128)(2,1)} %w_cross_ref.1) | copy-start | bytes 1572868
  32.3 42.8 %copy-start.4 = (bf16[256,256]{1,0:T(8,128)(2,1)S(1)}, bf16[256,256]{1,0:T(8,128)(2,1)}, u32[]{:S(2)}) copy-start(bf16[256,256]{1,0:T(8,128)(2,1)} %item_ref.1) | copy-start | bytes 393220

commit v5 on v4

--- a/solution.py
+++ b/solution.py
@@ -11,7 +11,6 @@
 LOW_BITS = 7
 LOW = 1 << LOW_BITS
 DEPTH = 256
-HALF = 8
 VMEM_LIMIT = 32 * 1024 * 1024
 
 
@@ -36,22 +35,15 @@
 
 def count_kernel(users, words_ref, *refs):
     counts_ref = refs[-1]
-    sources = words_ref.shape[0]
-    first_core = lax.rem(lax.axis_index("table"), 2) == 0
-    positions = 2 * words_ref.shape[2]
-    slots = positions // users
+    sources, _, positions = words_ref.shape
+    half = users // 2
     side_by_side = counts_ref.shape[2] // LOW
     highs = counts_ref.shape[0] // 2 * side_by_side
+    first_core = lax.rem(lax.axis_index("table"), 2) == 0
+    user_of = lax.broadcasted_iota(jnp.int32, (1, positions), 1) // (positions // half)
+    high_rows = lax.broadcasted_iota(jnp.int32, (highs * half, positions), 0).astype(jnp.int8)
     low_rows = lax.broadcasted_iota(jnp.int32, (LOW, positions), 0).astype(jnp.int8)
     one, zero = jnp.ones((), F8), jnp.zeros((), F8)
-    tiles = []
-    for first in range(0, positions, DEPTH):
-        groups = sorted({first // slots // HALF, (first + DEPTH - 1) // slots // HALF})
-        rows = len(groups) * HALF
-        middle = highs * rows // 2
-        user = (lax.broadcasted_iota(jnp.int32, (1, DEPTH), 1) + first) // slots - groups[0] * HALF
-        code_rows = lax.broadcasted_iota(jnp.int32, (highs * rows, DEPTH), 0) - middle
-        tiles.append((slice(first, first + DEPTH), groups, rows, user - middle, code_rows.astype(jnp.int8)))
 
     def count(source, carry):
         pair = words_ref[source]
@@ -59,24 +51,18 @@
         other = jnp.where(first_core, pair[1:], pair[:1])
         target = pl.ds(pl.multiple_of(source * users, users), users)
         for shard, words in enumerate((own, other)):
-            ids = jnp.concatenate([words & 0xFFFF, (words >> 16) & 0xFFFF], axis=1)
-            low = jnp.where(ids < highs * LOW, ids & (LOW - 1), -1).astype(jnp.int8)
-            high = (ids >> LOW_BITS) & (highs - 1)
-            low_hot = jnp.where(low == low_rows, one, zero)
-            found = {}
-            for piece, groups, rows, base, code_rows in tiles:
-                code = (high[:, piece] * rows + base).astype(jnp.int8)
-                high_hot = jnp.where(code == code_rows, one, zero)
-                counts = rows_by_rows(high_hot, low_hot[:, piece])
-                for part in range(highs):
-                    for i, group in enumerate(groups):
-                        start = part * rows + i * HALF
-                        found.setdefault((part, group), []).append(counts[start : start + HALF])
+            halves = []
+            for ids in (words & 0xFFFF, (words >> 16) & 0xFFFF):
+                low = jnp.where(ids < highs * LOW, ids & (LOW - 1), -1).astype(jnp.int8)
+                high = (((ids >> LOW_BITS) & (highs - 1)) * half + user_of).astype(jnp.int8)
+                high_hot = jnp.where(high == high_rows, one, zero)
+                low_hot = jnp.where(low == low_rows, one, zero)
+                halves.append(rows_by_rows(high_hot, low_hot))
             for part in range(highs):
-                sums = [sum(found[part, group][1:], found[part, group][0]) for group in range(users // HALF)]
+                rows = slice(part * half, (part + 1) * half)
                 lane = part % side_by_side * LOW
                 counts_ref[(shard * highs + part) // side_by_side, target, lane : lane + LOW] = jnp.concatenate(
-                    sums, axis=0
+                    [counts[rows] for counts in halves], axis=0
                 ).astype(BF16)
         return carry
 

time: 95.1 us -> 94.8 us (level)
  no operation moved by 1% of the time
where the time goes in v5:
time: 94.8 us; the launch traced here: 94.4 us
  blocking collectives  84 us (89%)
  Pallas kernels  6.44 us (7%)
  starting transfers between devices  1.92 us (2%)
  other arithmetic  1.11 us (1%)
    all_to_all x1, blocking collectives, body(): lax.all_to_all(words, 'table', split_axis=0, concat_axis=0, tiled=True, a...  25.7 us
    all_to_all x1, blocking collectives, body(): lax.all_to_all(jnp.broadcast_to(pooled_user[None], (samples, users, width...  25.7 us
    all_to_all x1, blocking collectives, body(): lax.all_to_all(per_user.reshape(samples, users, width), 'sample', split_a...  16.9 us
    all_to_all x1, blocking collectives, body(): lax.all_to_all(partials, 'table', split_axis=0, concat_axis=0, tiled=True...  15.8 us
    pallas_call x1, Pallas kernels, body(): kernel_call(lambda *refs: count_kernel(users, *refs), jax.ShapeDtypeStruc...  2.31 us
    pallas_call x1, Pallas kernels, body(): kernel_call(dense_kernel, (jax.ShapeDtypeStruct((1, imps), F32), jax.Shap...  2.02 us
    ppermute x1, starting transfers between devices, body(): lax.ppermute(table_rows, 'table', [(i, i ^ 1) for i in range(sources)])  1.92 us
  transfers between devices with their start and end apart: 1, of which 0 were waited for; matrix products, arithmetic and copies ran while one was open for 1% of the time, Pallas kernels for 3%

profile of v5, /device:TPU:8, one launch (start us, length us, event | category | flops | bytes accessed | tf_op | source)
XLA Modules:
  0.0 94.4 jit_solution(5410344472764002477)
XLA Ops:
  0.6 1.9 %collective-permute-start = (bf16[2048,256]{1,0:T(8,128)(2,1)}, bf16[2048,256]{1,0:T(8,128)(2,1)S(1)}, u32[]{:S(2)}, u32[]{:S(2)}) collective-permute-start(bf16[2048,256]{1,0:T(8,128)(2,1)} %own_ref.1), channel_id=1, source_target_pairs={{0,16},{16,0},{32,48},{48,32},{64,80},{80,64},{96,112},{112,96},{1... | collective-permute-start | bytes 3145736 | tf_op jit(solution)/shard_map/ppermute | solution.py:215
  2.6 1.0 %bitcast_select_fusion = s32[16,48,64]{2,1,0:T(8,128)S(1)} fusion(s32[16,64,48]{1,2,0:T(8,128)} %param.13, s32[16,64]{1,0:T(8,128)} %param.14), kind=kLoop, calls=%fused_computation.1 | loop fusion | flops 98304 | bytes 397312 | tf_op jit(solution)/shard_map/pack_ids/jit(_where)/select_n | solution.py:23
  3.6 0.0 copy-start.5
  3.6 0.0 copy-start.6
  3.6 0.0 copy-start.7
  3.7 0.0 copy-start.8
  3.7 0.0 copy-start.9
  3.7 0.0 copy-start.10
  3.7 0.1 pack_ids.1
  3.8 25.7 %all_to_all.20.refs_0_ = s32[32,2,384]{2,1,0:T(2,128)S(1)} all-to-all(s32[32,2,384]{2,1,0:T(2,128)S(1)} %pack_ids.1), channel_id=1, replica_groups={{0,32,64,96,128,160,192,224,256,288,320,352,384,416,448,480,512,544,576..., dimensions={0} | all-to-all | bytes 196608 | tf_op jit(solution)/shard_map/all_to_all | solution.py:216
  29.6 0.0 copy-done.5
  29.6 0.0 copy-done.6
  29.6 0.0 copy-done.7
  29.6 0.0 copy-done.8
  29.6 0.0 copy-done.9
  29.6 0.0 copy-done.10
  29.6 0.0 copy-start
  29.6 2.3 %count.1.counts_ref = bf16[16,512,256]{2,1,0:T(8,128)(2,1)S(1)} custom-call(s32[32,2,384]{2,1,0:T(2,128)S(1)} %all_to_all.20.refs_0_, s32[1,256]{1,0:T(1,128)S(1)} %bitcast.21, s32[1,256]{1,0:T(1,128)S(1)} %bitcast.23, f32[1,512]{1,0:T(1,128)S(1)} %bitcast.13, f32[1,512]{1,0:T(1,128)S(1)} %bitcast.15, f32[1,512]{1,0:T(1,128)S(1)} %bitcast.17, ...), custom_call_target="tpu_custom_call" | custom-call | flops 8589934592 | bytes 2097152 | tf_op jit(solution)/shard_map/count/pallas_call | solution.py:221
  31.9 0.0 copy-start.1
  31.9 0.0 copy-start.2
  32.0 0.0 copy-start.3
  32.0 0.0 copy-start.4
  32.0 0.0 collective-permute-done.other_ref
  32.0 0.0 copy-done
  32.0 1.2 %pool.1 = bf16[32,16,256]{2,1,0:T(8,128)(2,1)S(1)} custom-call(bf16[16,512,256]{2,1,0:T(8,128)(2,1)S(1)} %count.1.counts_ref, bf16[2048,256]{1,0:T(8,128)(2,1)S(1)} %copy-done, bf16[2048,256]{1,0:T(8,128)(2,1)S(1)} %collective-permute-done.other_ref), custom_call_target="tpu_custom_call" | custom-call | flops 1073741824 | bytes 2097152 | tf_op jit(solution)/shard_map/pool/pallas_call | solution.py:227
  33.3 15.8 %all_to_all.21 = bf16[32,16,256]{2,1,0:T(8,128)(2,1)S(1)} all-to-all(bf16[32,16,256]{2,1,0:T(8,128)(2,1)S(1)} %pool.1), channel_id=1, replica_groups={{0,32,64,96,128,160,192,224,256,288,320,352,384,416,448,480,512,544,576..., dimensions={0} | all-to-all | bytes 524288 | tf_op jit(solution)/shard_map/all_to_all | solution.py:231
  49.1 25.7 %all_to_all.22 = bf16[16,16,256]{2,1,0:T(8,128)(2,1)S(1)} all-to-all(bf16[16,16,256]{2,1,0:T(8,128)(2,1)S(1)} %broadcast_in_dim.12), channel_id=1, replica_groups=mesh['table'=64,'sample'=16] {'sample'}, dimensions={0} | all-to-all | bytes 262144 | tf_op jit(solution)/shard_map/all_to_all | solution.py:235
  74.8 0.0 copy-done.1
  74.8 0.0 copy-done.2
  74.8 0.0 copy-done.3
  74.8 0.0 copy-done.4
  74.8 2.0 %dense.1 = (f32[1,256]{1,0:T(1,128)S(1)}, f32[256,256]{1,0:T(8,128)S(1)}, bf16[256,256]{1,0:T(8,128)(2,1)S(1)}) custom-call(bf16[256,256]{1,0:T(8,128)(2,1)S(1)} %bitcast.11, s32[1,256]{1,0:T(1,128)S(1)} %bitcast.22, bf16[256,256]{1,0:T(8,128)(2,1)S(1)} %copy-done.4, s32[1,256]{1,0:T(1,128)S(1)} %bitcast.24, bf16[512,512]{1,0:T(8,128)(2,1)S(1)} %copy-done.1, ...), custom_call_target="tpu_custom_call" | custom-call | flops 1073741824 | bytes 2097152 | tf_op jit(solution)/shard_map/dense/pallas_call | solution.py:243
  76.8 16.9 %all_to_all.23.parts_ref = bf16[16,16,256]{2,1,0:T(8,128)(2,1)S(1)} all-to-all(bf16[16,16,256]{2,1,0:T(8,128)(2,1)S(1)} %bitcast.12), channel_id=1, replica_groups=mesh['table'=64,'sample'=16] {'sample'}, dimensions={0} | all-to-all | bytes 262144 | tf_op jit(solution)/shard_map/all_to_all | solution.py:264
  93.7 0.7 finish.1
  (4 shorter events, 0.1 us)
Async XLA Ops:
  0.6 31.4 %collective-permute-start = (bf16[2048,256]{1,0:T(8,128)(2,1)}, bf16[2048,256]{1,0:T(8,128)(2,1)S(1)}, u32[]{:S(2)}, u32[]{:S(2)}) collective-permute-start(bf16[2048,256]{1,0:T(8,128)(2,1)} %own_ref.1), channel_id=1, source_target_pairs={{0,16},{16,0},{32,48},{48,32},{64,80},{80,64},{96,112},{112,96},{1... | collective-permute-start | bytes 3145736 | tf_op jit(solution)/shard_map/ppermute | solution.py:215
  3.6 25.9 %copy-start.5 = (f32[512]{0:T(512)S(1)}, f32[512]{0:T(512)}, u32[]{:S(2)}) copy-start(f32[512]{0:T(512)} %param.20) | copy-start | bytes 6148
  3.6 25.9 %copy-start.6 = (f32[512]{0:T(512)S(1)}, f32[512]{0:T(512)}, u32[]{:S(2)}) copy-start(f32[512]{0:T(512)} %param.23) | copy-start | bytes 6148
  3.6 25.9 %copy-start.7 = (f32[512]{0:T(512)S(1)}, f32[512]{0:T(512)}, u32[]{:S(2)}) copy-start(f32[512]{0:T(512)} %param.24) | copy-start | bytes 6148
  3.7 25.9 %copy-start.8 = (f32[512]{0:T(512)S(1)}, f32[512]{0:T(512)}, u32[]{:S(2)}) copy-start(f32[512]{0:T(512)} %param.25) | copy-start | bytes 6148
  3.7 25.9 %copy-start.9 = (s32[256]{0:T(256)S(1)}, s32[256]{0:T(256)}, u32[]{:S(2)}) copy-start(s32[256]{0:T(256)} %param.16) | copy-start | bytes 3076
  3.7 25.9 %copy-start.10 = (s32[256]{0:T(256)S(1)}, s32[256]{0:T(256)}, u32[]{:S(2)}) copy-start(s32[256]{0:T(256)} %param.18) | copy-start | bytes 3076
  29.6 2.4 %copy-start = (bf16[2048,256]{1,0:T(8,128)(2,1)S(1)}, bf16[2048,256]{1,0:T(8,128)(2,1)}, u32[]{:S(2)}) copy-start(bf16[2048,256]{1,0:T(8,128)(2,1)} %own_ref.1) | copy-start | bytes 3145732
  31.9 42.9 %copy-start.1 = (bf16[512,512]{1,0:T(8,128)(2,1)S(1)}, bf16[512,512]{1,0:T(8,128)(2,1)}, u32[]{:S(2)}) copy-start(bf16[512,512]{1,0:T(8,128)(2,1)} %w_hidden_ref.1) | copy-start | bytes 1572868
  31.9 42.8 %copy-start.2 = (bf16[512,512]{1,0:T(8,128)(2,1)S(1)}, bf16[512,512]{1,0:T(8,128)(2,1)}, u32[]{:S(2)}) copy-start(bf16[512,512]{1,0:T(8,128)(2,1)} %w_back_ref.1) | copy-start | bytes 1572868
  32.0 42.8 %copy-start.3 = (bf16[512,512]{1,0:T(8,128)(2,1)S(1)}, bf16[512,512]{1,0:T(8,128)(2,1)}, u32[]{:S(2)}) copy-start(bf16[512,512]{1,0:T(8,128)(2,1)} %w_cross_ref.1) | copy-start | bytes 1572868
  32.0 42.8 %copy-start.4 = (bf16[256,256]{1,0:T(8,128)(2,1)S(1)}, bf16[256,256]{1,0:T(8,128)(2,1)}, u32[]{:S(2)}) copy-start(bf16[256,256]{1,0:T(8,128)(2,1)} %item_ref.1) | copy-start | bytes 393220

commit v6 on v5

--- a/solution.py
+++ b/solution.py
@@ -39,7 +39,7 @@
     half = users // 2
     side_by_side = counts_ref.shape[2] // LOW
     highs = counts_ref.shape[0] // 2 * side_by_side
-    first_core = lax.rem(lax.axis_index("table"), 2) == 0
+    core = lax.rem(lax.axis_index("table"), 2)
     user_of = lax.broadcasted_iota(jnp.int32, (1, positions), 1) // (positions // half)
     high_rows = lax.broadcasted_iota(jnp.int32, (highs * half, positions), 0).astype(jnp.int8)
     low_rows = lax.broadcasted_iota(jnp.int32, (LOW, positions), 0).astype(jnp.int8)
@@ -47,21 +47,22 @@
 
     def count(source, carry):
         pair = words_ref[source]
-        own = jnp.where(first_core, pair[:1], pair[1:])
-        other = jnp.where(first_core, pair[1:], pair[:1])
         target = pl.ds(pl.multiple_of(source * users, users), users)
-        for shard, words in enumerate((own, other)):
+        codes = []
+        for ids in (pair & 0xFFFF, (pair >> 16) & 0xFFFF):
+            low = jnp.where(ids < highs * LOW, ids & (LOW - 1), -1)
+            codes.append((((ids >> LOW_BITS) & (highs - 1)) * half + user_of, low))
+        for shard in range(2):
             halves = []
-            for ids in (words & 0xFFFF, (words >> 16) & 0xFFFF):
-                low = jnp.where(ids < highs * LOW, ids & (LOW - 1), -1).astype(jnp.int8)
-                high = (((ids >> LOW_BITS) & (highs - 1)) * half + user_of).astype(jnp.int8)
-                high_hot = jnp.where(high == high_rows, one, zero)
-                low_hot = jnp.where(low == low_rows, one, zero)
+            for high, low in codes:
+                high_hot = jnp.where(high[shard : shard + 1].astype(jnp.int8) == high_rows, one, zero)
+                low_hot = jnp.where(low[shard : shard + 1].astype(jnp.int8) == low_rows, one, zero)
                 halves.append(rows_by_rows(high_hot, low_hot))
+            first_part = (core ^ shard) * (highs // side_by_side)
             for part in range(highs):
                 rows = slice(part * half, (part + 1) * half)
                 lane = part % side_by_side * LOW
-                counts_ref[(shard * highs + part) // side_by_side, target, lane : lane + LOW] = jnp.concatenate(
+                counts_ref[first_part + part // side_by_side, target, lane : lane + LOW] = jnp.concatenate(
                     [counts[rows] for counts in halves], axis=0
                 ).astype(BF16)
         return carry

time: 94.8 us -> 94.7 us (level)
  no operation moved by 1% of the time
where the time goes in v6:
time: 94.7 us; the launch traced here: 94.4 us
  blocking collectives  84 us (89%)
  Pallas kernels  6.43 us (7%)
  starting transfers between devices  1.92 us (2%)
  other arithmetic  1.11 us (1%)
    all_to_all x1, blocking collectives, body(): lax.all_to_all(words, 'table', split_axis=0, concat_axis=0, tiled=True, a...  25.7 us
    all_to_all x1, blocking collectives, body(): lax.all_to_all(jnp.broadcast_to(pooled_user[None], (samples, users, width...  25.7 us
    all_to_all x1, blocking collectives, body(): lax.all_to_all(per_user.reshape(samples, users, width), 'sample', split_a...  16.8 us
    all_to_all x1, blocking collectives, body(): lax.all_to_all(partials, 'table', split_axis=0, concat_axis=0, tiled=True...  15.8 us
    pallas_call x1, Pallas kernels, body(): kernel_call(lambda *refs: count_kernel(users, *refs), jax.ShapeDtypeStruc...  2.29 us
    pallas_call x1, Pallas kernels, body(): kernel_call(dense_kernel, (jax.ShapeDtypeStruct((1, imps), F32), jax.Shap...  2.02 us
    ppermute x1, starting transfers between devices, body(): lax.ppermute(table_rows, 'table', [(i, i ^ 1) for i in range(sources)])  1.92 us
  transfers between devices with their start and end apart: 1, of which 0 were waited for; matrix products, arithmetic and copies ran while one was open for 1% of the time, Pallas kernels for 3%

profile of v6, /device:TPU:8, one launch (start us, length us, event | category | flops | bytes accessed | tf_op | source)
XLA Modules:
  0.0 94.4 jit_solution(17488310354856920281)
XLA Ops:
  0.6 1.9 %collective-permute-start = (bf16[2048,256]{1,0:T(8,128)(2,1)}, bf16[2048,256]{1,0:T(8,128)(2,1)S(1)}, u32[]{:S(2)}, u32[]{:S(2)}) collective-permute-start(bf16[2048,256]{1,0:T(8,128)(2,1)} %own_ref.1), channel_id=1, source_target_pairs={{0,16},{16,0},{32,48},{48,32},{64,80},{80,64},{96,112},{112,96},{1... | collective-permute-start | bytes 3145736 | tf_op jit(solution)/shard_map/ppermute | solution.py:216
  2.6 1.0 %bitcast_select_fusion = s32[16,48,64]{2,1,0:T(8,128)S(1)} fusion(s32[16,64,48]{1,2,0:T(8,128)} %param.13, s32[16,64]{1,0:T(8,128)} %param.14), kind=kLoop, calls=%fused_computation.1 | loop fusion | flops 98304 | bytes 397312 | tf_op jit(solution)/shard_map/pack_ids/jit(_where)/select_n | solution.py:23
  3.6 0.0 copy-start.5
  3.6 0.0 copy-start.6
  3.6 0.0 copy-start.7
  3.7 0.0 copy-start.8
  3.7 0.0 copy-start.9
  3.7 0.0 copy-start.10
  3.7 0.1 pack_ids.1
  3.8 25.7 %all_to_all.20.refs_0_ = s32[32,2,384]{2,1,0:T(2,128)S(1)} all-to-all(s32[32,2,384]{2,1,0:T(2,128)S(1)} %pack_ids.1), channel_id=1, replica_groups={{0,32,64,96,128,160,192,224,256,288,320,352,384,416,448,480,512,544,576..., dimensions={0} | all-to-all | bytes 196608 | tf_op jit(solution)/shard_map/all_to_all | solution.py:217
  29.6 0.0 copy-done.5
  29.6 0.0 copy-done.6
  29.6 0.0 copy-done.7
  29.6 0.0 copy-done.8
  29.6 0.0 copy-done.9
  29.6 0.0 copy-done.10
  29.6 0.0 copy-start
  29.6 2.3 %count.1.counts_ref = bf16[16,512,256]{2,1,0:T(8,128)(2,1)S(1)} custom-call(s32[32,2,384]{2,1,0:T(2,128)S(1)} %all_to_all.20.refs_0_, s32[1,256]{1,0:T(1,128)S(1)} %bitcast.21, s32[1,256]{1,0:T(1,128)S(1)} %bitcast.23, f32[1,512]{1,0:T(1,128)S(1)} %bitcast.13, f32[1,512]{1,0:T(1,128)S(1)} %bitcast.15, f32[1,512]{1,0:T(1,128)S(1)} %bitcast.17, ...), custom_call_target="tpu_custom_call" | custom-call | flops 8589934592 | bytes 2097152 | tf_op jit(solution)/shard_map/count/pallas_call | solution.py:222
  31.9 0.0 copy-start.1
  31.9 0.0 copy-start.2
  31.9 0.0 copy-start.3
  32.0 0.0 copy-start.4
  32.0 0.0 collective-permute-done.other_ref
  32.0 0.0 copy-done
  32.0 1.2 %pool.1 = bf16[32,16,256]{2,1,0:T(8,128)(2,1)S(1)} custom-call(bf16[16,512,256]{2,1,0:T(8,128)(2,1)S(1)} %count.1.counts_ref, bf16[2048,256]{1,0:T(8,128)(2,1)S(1)} %copy-done, bf16[2048,256]{1,0:T(8,128)(2,1)S(1)} %collective-permute-done.other_ref), custom_call_target="tpu_custom_call" | custom-call | flops 1073741824 | bytes 2097152 | tf_op jit(solution)/shard_map/pool/pallas_call | solution.py:228
  33.2 15.8 %all_to_all.21 = bf16[32,16,256]{2,1,0:T(8,128)(2,1)S(1)} all-to-all(bf16[32,16,256]{2,1,0:T(8,128)(2,1)S(1)} %pool.1), channel_id=1, replica_groups={{0,32,64,96,128,160,192,224,256,288,320,352,384,416,448,480,512,544,576..., dimensions={0} | all-to-all | bytes 524288 | tf_op jit(solution)/shard_map/all_to_all | solution.py:232
  49.1 25.7 %all_to_all.22 = bf16[16,16,256]{2,1,0:T(8,128)(2,1)S(1)} all-to-all(bf16[16,16,256]{2,1,0:T(8,128)(2,1)S(1)} %broadcast_in_dim.12), channel_id=1, replica_groups=mesh['table'=64,'sample'=16] {'sample'}, dimensions={0} | all-to-all | bytes 262144 | tf_op jit(solution)/shard_map/all_to_all | solution.py:236
  74.8 0.0 copy-done.1
  74.8 0.0 copy-done.2
  74.8 0.0 copy-done.3
  74.8 0.0 copy-done.4
  74.8 2.0 %dense.1 = (f32[1,256]{1,0:T(1,128)S(1)}, f32[256,256]{1,0:T(8,128)S(1)}, bf16[256,256]{1,0:T(8,128)(2,1)S(1)}) custom-call(bf16[256,256]{1,0:T(8,128)(2,1)S(1)} %bitcast.11, s32[1,256]{1,0:T(1,128)S(1)} %bitcast.22, bf16[256,256]{1,0:T(8,128)(2,1)S(1)} %copy-done.4, s32[1,256]{1,0:T(1,128)S(1)} %bitcast.24, bf16[512,512]{1,0:T(8,128)(2,1)S(1)} %copy-done.1, ...), custom_call_target="tpu_custom_call" | custom-call | flops 1073741824 | bytes 2097152 | tf_op jit(solution)/shard_map/dense/pallas_call | solution.py:244
  76.8 16.8 %all_to_all.23.parts_ref = bf16[16,16,256]{2,1,0:T(8,128)(2,1)S(1)} all-to-all(bf16[16,16,256]{2,1,0:T(8,128)(2,1)S(1)} %bitcast.12), channel_id=1, replica_groups=mesh['table'=64,'sample'=16] {'sample'}, dimensions={0} | all-to-all | bytes 262144 | tf_op jit(solution)/shard_map/all_to_all | solution.py:265
  93.7 0.7 finish.1
  (4 shorter events, 0.1 us)
Async XLA Ops:
  0.6 31.3 %collective-permute-start = (bf16[2048,256]{1,0:T(8,128)(2,1)}, bf16[2048,256]{1,0:T(8,128)(2,1)S(1)}, u32[]{:S(2)}, u32[]{:S(2)}) collective-permute-start(bf16[2048,256]{1,0:T(8,128)(2,1)} %own_ref.1), channel_id=1, source_target_pairs={{0,16},{16,0},{32,48},{48,32},{64,80},{80,64},{96,112},{112,96},{1... | collective-permute-start | bytes 3145736 | tf_op jit(solution)/shard_map/ppermute | solution.py:216
  3.6 25.9 %copy-start.5 = (f32[512]{0:T(512)S(1)}, f32[512]{0:T(512)}, u32[]{:S(2)}) copy-start(f32[512]{0:T(512)} %param.20) | copy-start | bytes 6148
  3.6 25.9 %copy-start.6 = (f32[512]{0:T(512)S(1)}, f32[512]{0:T(512)}, u32[]{:S(2)}) copy-start(f32[512]{0:T(512)} %param.23) | copy-start | bytes 6148
  3.6 25.9 %copy-start.7 = (f32[512]{0:T(512)S(1)}, f32[512]{0:T(512)}, u32[]{:S(2)}) copy-start(f32[512]{0:T(512)} %param.24) | copy-start | bytes 6148
  3.7 25.9 %copy-start.8 = (f32[512]{0:T(512)S(1)}, f32[512]{0:T(512)}, u32[]{:S(2)}) copy-start(f32[512]{0:T(512)} %param.25) | copy-start | bytes 6148
  3.7 25.9 %copy-start.9 = (s32[256]{0:T(256)S(1)}, s32[256]{0:T(256)}, u32[]{:S(2)}) copy-start(s32[256]{0:T(256)} %param.16) | copy-start | bytes 3076
  3.7 25.9 %copy-start.10 = (s32[256]{0:T(256)S(1)}, s32[256]{0:T(256)}, u32[]{:S(2)}) copy-start(s32[256]{0:T(256)} %param.18) | copy-start | bytes 3076
  29.6 2.4 %copy-start = (bf16[2048,256]{1,0:T(8,128)(2,1)S(1)}, bf16[2048,256]{1,0:T(8,128)(2,1)}, u32[]{:S(2)}) copy-start(bf16[2048,256]{1,0:T(8,128)(2,1)} %own_ref.1) | copy-start | bytes 3145732
  31.9 42.9 %copy-start.1 = (bf16[512,512]{1,0:T(8,128)(2,1)S(1)}, bf16[512,512]{1,0:T(8,128)(2,1)}, u32[]{:S(2)}) copy-start(bf16[512,512]{1,0:T(8,128)(2,1)} %w_hidden_ref.1) | copy-start | bytes 1572868
  31.9 42.8 %copy-start.2 = (bf16[512,512]{1,0:T(8,128)(2,1)S(1)}, bf16[512,512]{1,0:T(8,128)(2,1)}, u32[]{:S(2)}) copy-start(bf16[512,512]{1,0:T(8,128)(2,1)} %w_back_ref.1) | copy-start | bytes 1572868
  31.9 42.8 %copy-start.3 = (bf16[512,512]{1,0:T(8,128)(2,1)S(1)}, bf16[512,512]{1,0:T(8,128)(2,1)}, u32[]{:S(2)}) copy-start(bf16[512,512]{1,0:T(8,128)(2,1)} %w_cross_ref.1) | copy-start | bytes 1572868
  32.0 42.8 %copy-start.4 = (bf16[256,256]{1,0:T(8,128)(2,1)S(1)}, bf16[256,256]{1,0:T(8,128)(2,1)}, u32[]{:S(2)}) copy-start(bf16[256,256]{1,0:T(8,128)(2,1)} %item_ref.1) | copy-start | bytes 393220
